TPU v7x, 32 devices: a whole 2x2x4 slice. The times are simulated.
32 devices in a mesh: dp: 8 (over z, x), tensor: 4 (over y, core).
Axes of the slice: x: 2, y: 2, z: 4, core: 2. Of those that a mesh axis runs over, the one named last changes fastest.
Arguments:
- hidden_in: bfloat16 [16384, 768], P(('dp', 'tensor')), may hold values from -6 to 6
- out_grad: float32 [16384, 768], P(('dp', 'tensor')), may hold values from -11 to 11
- positions: int32 [16384], P('dp'), may hold values from 0 to 2047, as said below
- query_weight: float32 [2, 768, 768], P(None, 'dp', 'tensor'), may hold values from -0.21875 to 0.21875
- keyval_weight: float32 [768, 128], P('dp'), may hold values from -0.21875 to 0.21875
- output_weight: float32 [2, 768, 768], P(None, 'tensor', 'dp'), may hold values from -0.625 to 0.625
- up_weight: float32 [2, 768, 3072], P(None, 'dp', 'tensor'), may hold values from -0.4330127 to 0.4330127
- down_weight: float32 [2, 3072, 768], P(None, 'tensor', 'dp'), may hold values from -0.109375 to 0.109375
- norm_params: float32 [2, 4, 768], P(None, None, 'dp'), may hold values from -2 to 3
- query_first: float32 [2, 768, 768], P(None, 'dp', 'tensor'), may hold values from -768 to 768
- query_second: float32 [2, 768, 768], P(None, 'dp', 'tensor'), may hold values from 8192 to 65536
- keyval_first: float32 [768, 128], P('dp'), may hold values from -2048 to 2048
- keyval_second: float32 [768, 128], P('dp'), may hold values from 65536 to 524288
- output_first: float32 [2, 768, 768], P(None, 'tensor', 'dp'), may hold values from -384 to 384
- output_second: float32 [2, 768, 768], P(None, 'tensor', 'dp'), may hold values from 2048 to 16384
- up_first: float32 [2, 768, 3072], P(None, 'dp', 'tensor'), may hold values from -384 to 384
- up_second: float32 [2, 768, 3072], P(None, 'dp', 'tensor'), may hold values from 2048 to 16384
- down_first: float32 [2, 3072, 768], P(None, 'tensor', 'dp'), may hold values from -448 to 448
- down_second: float32 [2, 3072, 768], P(None, 'tensor', 'dp'), may hold values from 3276.8 to 26214.4
- norm_first: float32 [2, 4, 768], P(None, None, 'dp'), may hold values from -768 to 768
- norm_second: float32 [2, 4, 768], P(None, None, 'dp'), may hold values from 8192 to 65536
Outputs:
- block_out: float32 [16384, 768], P(('dp', 'tensor'))
- input_grad: float32 [16384, 768], P(('dp', 'tensor'))
- query_first_next: float32 [2, 768, 768], P(None, 'dp', 'tensor')
- query_second_next: float32 [2, 768, 768], P(None, 'dp', 'tensor')
- query_next: float32 [2, 768, 768], P(None, 'dp', 'tensor')
- query_low: bfloat16 [2, 768, 768], P(None, 'dp', 'tensor')
- keyval_first_next: float32 [768, 128], P('dp')
- keyval_second_next: float32 [768, 128], P('dp')
- keyval_next: float32 [768, 128], P('dp')
- keyval_low: bfloat16 [768, 128], P('dp')
- output_first_next: float32 [2, 768, 768], P(None, 'tensor', 'dp')
- output_second_next: float32 [2, 768, 768], P(None, 'tensor', 'dp')
- output_next: float32 [2, 768, 768], P(None, 'tensor', 'dp')
- output_low: bfloat16 [2, 768, 768], P(None, 'tensor', 'dp')
- up_first_next: float32 [2, 768, 3072], P(None, 'dp', 'tensor')
- up_second_next: float32 [2, 768, 3072], P(None, 'dp', 'tensor')
- up_next: float32 [2, 768, 3072], P(None, 'dp', 'tensor')
- up_low: bfloat16 [2, 768, 3072], P(None, 'dp', 'tensor')
- down_first_next: float32 [2, 3072, 768], P(None, 'tensor', 'dp')
- down_second_next: float32 [2, 3072, 768], P(None, 'tensor', 'dp')
- down_next: float32 [2, 3072, 768], P(None, 'tensor', 'dp')
- down_low: bfloat16 [2, 3072, 768], P(None, 'tensor', 'dp')
- norm_first_next: float32 [2, 4, 768], P(None, None, 'dp')
- norm_second_next: float32 [2, 4, 768], P(None, None, 'dp')
- norm_next: float32 [2, 4, 768], P(None, None, 'dp')
- norm_low: bfloat16 [2, 4, 768], P(None, None, 'dp')
- update_norms: float32 [17], replicated
- trust_ratios: float32 [17], replicated
Inputs may be any that keep to these rules, and one draw needn't show every extreme that they name: Within each sequence of 2048 rows positions count up by one from 0 at its first row and restart at 0 where a packed document begins; one sequence, which one drawn from the seed, holds a single document, so its last row has position 2047.
All inputs are finite; a program needn't handle non-finite values.
Results may differ from a plain program's by a relative error of at most 0.024.
The roundings to bfloat16 on the way count: a program that leaves them out, or rounds other values in their place, can miss the bound.
Values may be sent and summed in bfloat16 or wider, within the bound.
A program may use at most 192 MiB of HBM per device.

v0:
```python
from functools import partial
import math

import jax
import jax.numpy as jnp
from jax import lax
from jax.sharding import PartitionSpec as P

HD = 64
ROT = 16
STEP = 5


NORM_EPSILON = 1e-05
BETA_FIRST = 0.5
BETA_SECOND = 0.55
ADAM_EPSILON = 1e-06
WEIGHT_DECAY = 0.01
LEARN_RATE = 0.5


def standardize(values):
    center = values - jnp.mean(values, axis=-1, keepdims=True)
    spread = jnp.mean(center * center, axis=-1, keepdims=True)
    return center * lax.rsqrt(spread + NORM_EPSILON)


def layer_norm(values, gain, bias):
    return standardize(values) * gain + bias


def normed_both(state, params):
    return (layer_norm(state, params[0], params[1]), layer_norm(state, params[2], params[3]))


def spread_rows(centered, normed_attn, params):
    normed_mlp = (centered * params[2] + params[3]).astype(jnp.bfloat16)
    attn_full, mlp_full = (
        lax.all_gather(normed_attn, "tensor", axis=0, tiled=True),
        lax.all_gather(normed_mlp, "tensor", axis=0, tiled=True),
    )
    return (attn_full, mlp_full, None)


def angles(places):
    steps = jnp.arange(ROT // 2).astype(jnp.float32)
    inverse = jnp.exp(steps * (-2.0 * math.log(10000.0) / ROT))
    phase = places.astype(jnp.float32)[:, None] * (0.25 * inverse)[None, :]
    return (jnp.cos(phase), jnp.sin(phase))


def rotate(values, cosine, sine):
    half = ROT // 2
    first = values[..., :half]
    second = values[..., half:ROT]
    cos_rows = cosine[:, None, :]
    sin_rows = sine[:, None, :]
    return jnp.concatenate(
        [
            first * cos_rows - second * sin_rows,
            second * cos_rows + first * sin_rows,
            values[..., ROT:],
        ],
        axis=-1,
    )


def rotate_back(grads, cosine, sine):
    half = ROT // 2
    first = grads[..., :half]
    second = grads[..., half:ROT]
    cos_rows = cosine[:, None, :]
    sin_rows = sine[:, None, :]
    return jnp.concatenate(
        [
            first * cos_rows + second * sin_rows,
            second * cos_rows - first * sin_rows,
            grads[..., ROT:],
        ],
        axis=-1,
    )


def masked_scores(query_block, keys, start):
    scores = jnp.einsum(
        "qhd,kd->hqk", query_block, keys, preferred_element_type=jnp.float32
    ) * query_block.shape[2] ** (-0.5)
    rows = start + jnp.arange(query_block.shape[0])
    columns = jnp.arange(keys.shape[0])
    return jnp.where((columns[None, :] <= rows[:, None])[None], scores, -1e30)


def attention_forward(query, keys, values):
    length = query.shape[0]
    block = min(512, length)

    def one(start):
        query_block = lax.dynamic_slice_in_dim(query, start, block, 0)
        scores = masked_scores(query_block, keys, start)
        peak = jnp.max(scores, axis=-1, keepdims=True)
        weights = jnp.exp(scores - peak)
        total = jnp.sum(weights, axis=-1, keepdims=True)
        probs = (weights / total).astype(jnp.bfloat16)
        attended = jnp.einsum("hqk,kd->qhd", probs, values, preferred_element_type=jnp.float32)
        return (attended.astype(jnp.bfloat16), peak + jnp.log(total))

    attended, logsum = lax.map(one, jnp.arange(length // block) * block)
    return (attended.reshape(length, -1), logsum)


def attention_backward(query, keys, values, logsum, grad_attended):
    length, heads_here, head = query.shape
    block = min(512, length)
    scale = head ** (-0.5)
    grad_rows = grad_attended.reshape(length, heads_here, head)

    def one(carry, index):
        key_total, value_total = carry
        start = index * block
        query_block = lax.dynamic_slice_in_dim(query, start, block, 0)
        grad_block = lax.dynamic_slice_in_dim(grad_rows, start, block, 0)
        probs = jnp.exp(masked_scores(query_block, keys, start) - logsum[index])
        probs_low = probs.astype(jnp.bfloat16)
        attended = jnp.einsum(
            "hqk,kd->qhd", probs_low, values, preferred_element_type=jnp.float32
        ).astype(jnp.bfloat16)
        grad_probs = jnp.einsum(
            "qhd,kd->hqk", grad_block, values, preferred_element_type=jnp.float32
        )
        inner = jnp.sum(probs * grad_probs, axis=-1, keepdims=True)
        grad_scores = (probs * (grad_probs - inner)).astype(jnp.bfloat16)
        grad_query = (
            jnp.einsum("hqk,kd->qhd", grad_scores, keys, preferred_element_type=jnp.float32) * scale
        )
        key_total = (
            key_total
            + jnp.einsum(
                "hqk,qhd->kd", grad_scores, query_block, preferred_element_type=jnp.float32
            )
            * scale
        )
        value_total = value_total + jnp.einsum(
            "hqk,qhd->kd", probs_low, grad_block, preferred_element_type=jnp.float32
        )
        return ((key_total, value_total), (attended, grad_query))

    empty = jnp.zeros((length, head), jnp.float32)
    (key_grad, value_grad), (attended, grad_query) = lax.scan(
        one, (empty, empty), jnp.arange(length // block)
    )
    return (
        attended.reshape(length, heads_here * head),
        grad_query.reshape(length, heads_here, head),
        key_grad,
        value_grad,
    )


def param_squares(arrays, leader):
    query, keyval, output, upward, downward, norms = arrays
    return jnp.concatenate(
        [
            jnp.sum(query * query, axis=(1, 2)),
            (jnp.sum(keyval * keyval) * leader)[None],
            jnp.sum(output * output, axis=(1, 2)),
            jnp.sum(upward * upward, axis=(1, 2)),
            jnp.sum(downward * downward, axis=(1, 2)),
            jnp.sum(norms * norms, axis=2).reshape(8) * leader,
        ]
    )


def lamb_parts(weight, first, second, grad):
    first_new = BETA_FIRST * first + (1.0 - BETA_FIRST) * grad
    second_new = BETA_SECOND * second + (1.0 - BETA_SECOND) * grad * grad
    update = (
        first_new
        / (1.0 - BETA_FIRST**STEP)
        / (jnp.sqrt(second_new / (1.0 - BETA_SECOND**STEP)) + ADAM_EPSILON)
        + WEIGHT_DECAY * weight
    )
    return (first_new, second_new, update)


def apply_trust(masters, updates, trust):
    factors = (
        trust[0:2][:, None, None],
        trust[2],
        trust[3:5][:, None, None],
        trust[5:7][:, None, None],
        trust[7:9][:, None, None],
        trust[9:17].reshape(2, 4, 1),
    )
    return tuple(
        (
            weight - LEARN_RATE * factor * update
            for weight, factor, update in zip(masters, factors, updates)
        )
    )


def shards(
    hidden_in,
    out_grad,
    positions,
    query_weight,
    keyval_weight,
    output_weight,
    up_weight,
    down_weight,
    norm_params,
    query_first,
    query_second,
    keyval_first,
    keyval_second,
    output_first,
    output_second,
    up_first,
    up_second,
    down_first,
    down_second,
    norm_first,
    norm_second,
):
    masters = (query_weight, keyval_weight, output_weight, up_weight, down_weight, norm_params)
    leader = (lax.axis_index("tensor") == 0).astype(jnp.float32)
    query_full, keyval_full, output_full, up_full, down_full, norm_full = (
        lax.all_gather(query_weight.astype(jnp.bfloat16), "dp", axis=1, tiled=True),
        lax.all_gather(keyval_weight.astype(jnp.bfloat16), "dp", axis=0, tiled=True),
        lax.all_gather(output_weight.astype(jnp.bfloat16), "dp", axis=2, tiled=True),
        lax.all_gather(up_weight.astype(jnp.bfloat16), "dp", axis=1, tiled=True),
        lax.all_gather(down_weight.astype(jnp.bfloat16), "dp", axis=2, tiled=True),
        lax.all_gather(norm_params.astype(jnp.bfloat16), "dp", axis=2, tiled=True),
    )
    norm_full = norm_full.astype(jnp.float32)
    cosine, sine = angles(positions)
    length = positions.shape[0]
    current = hidden_in.astype(jnp.float32)
    keys = None
    values = None
    saved = []
    for layer in range(2):
        params = norm_full[layer]
        centered = standardize(current)
        normed_attn = (centered * params[0] + params[1]).astype(jnp.bfloat16)
        attn_full, mlp_full, centered_full = spread_rows(centered, normed_attn, params)
        query_lin = jnp.dot(attn_full, query_full[layer], preferred_element_type=jnp.float32)
        query = rotate(query_lin.reshape(length, -1, HD), cosine, sine).astype(jnp.bfloat16)
        if keys is None:
            shared = jnp.dot(attn_full, keyval_full, preferred_element_type=jnp.float32)
            keys = rotate(shared[:, None, :HD], cosine, sine)[:, 0].astype(jnp.bfloat16)
            values = shared[:, HD:].astype(jnp.bfloat16)
        attended, logsum = attention_forward(query, keys, values)
        active = jax.nn.gelu(
            jnp.dot(mlp_full, up_full[layer], preferred_element_type=jnp.float32), approximate=False
        ).astype(jnp.bfloat16)
        term = jnp.dot(attended, output_full[layer], preferred_element_type=jnp.float32) + jnp.dot(
            active, down_full[layer], preferred_element_type=jnp.float32
        )
        kept = None
        saved.append((current, centered, normed_attn, kept, logsum))
        current = current + lax.psum_scatter(term, "tensor", scatter_dimension=0, tiled=True)
    grad_state = out_grad
    key_grad = jnp.zeros((length, HD), jnp.float32)
    value_grad = jnp.zeros((length, HD), jnp.float32)
    query_grads = [None, None]
    output_grads = [None, None]
    up_grads = [None, None]
    down_grads = [None, None]
    norm_grads = [None, None]
    keyval_grad = None
    for layer in (1, 0):
        state, centered, normed_attn, kept, logsum = saved[layer]
        params = norm_full[layer]
        grad_full = lax.all_gather(grad_state.astype(jnp.bfloat16), "tensor", axis=0, tiled=True)
        attn_full, mlp_full, centered_full = spread_rows(centered, normed_attn, params)
        pre = jnp.dot(mlp_full, up_full[layer], preferred_element_type=jnp.float32)
        active, gelu_back = jax.vjp(partial(jax.nn.gelu, approximate=False), pre)
        active_low = active.astype(jnp.bfloat16)
        down_grads[layer] = jnp.einsum(
            "lf,ld->fd", active_low, grad_full, preferred_element_type=jnp.float32
        )
        grad_active = jnp.einsum(
            "ld,fd->lf", grad_full, down_full[layer], preferred_element_type=jnp.float32
        )
        grad_pre = gelu_back(grad_active)[0].astype(jnp.bfloat16)
        up_grads[layer] = jnp.einsum(
            "ld,lf->df", mlp_full, grad_pre, preferred_element_type=jnp.float32
        )
        mlp_grad = jnp.einsum(
            "lf,df->ld", grad_pre, up_full[layer], preferred_element_type=jnp.float32
        )
        query_lin = jnp.dot(attn_full, query_full[layer], preferred_element_type=jnp.float32)
        query = rotate(query_lin.reshape(length, -1, HD), cosine, sine).astype(jnp.bfloat16)
        grad_attended = jnp.einsum(
            "ld,hd->lh", grad_full, output_full[layer], preferred_element_type=jnp.float32
        ).astype(jnp.bfloat16)
        attended, grad_rot, key_part, value_part = attention_backward(
            query, keys, values, logsum, grad_attended
        )
        output_grads[layer] = jnp.einsum(
            "lh,ld->hd", attended, grad_full, preferred_element_type=jnp.float32
        )
        key_grad = key_grad + key_part
        value_grad = value_grad + value_part
        grad_query = rotate_back(grad_rot, cosine, sine).reshape(length, -1).astype(jnp.bfloat16)
        query_grads[layer] = jnp.einsum(
            "ld,lh->dh", attn_full, grad_query, preferred_element_type=jnp.float32
        )
        attn_grad = jnp.einsum(
            "lh,dh->ld", grad_query, query_full[layer], preferred_element_type=jnp.float32
        )
        shared_grad = None
        if layer == 0:
            shared_grad = jnp.concatenate(
                [rotate_back(key_grad[:, None, :], cosine, sine)[:, 0], value_grad], axis=1
            )
        if layer == 1:
            attn_local, mlp_local = (
                lax.psum_scatter(
                    attn_grad.astype(jnp.bfloat16), "tensor", scatter_dimension=0, tiled=True
                ).astype(jnp.float32),
                lax.psum_scatter(
                    mlp_grad.astype(jnp.bfloat16), "tensor", scatter_dimension=0, tiled=True
                ).astype(jnp.float32),
            )
        else:
            attn_local, mlp_local, shared_local = (
                lax.psum_scatter(
                    attn_grad.astype(jnp.bfloat16), "tensor", scatter_dimension=0, tiled=True
                ).astype(jnp.float32),
                lax.psum_scatter(
                    mlp_grad.astype(jnp.bfloat16), "tensor", scatter_dimension=0, tiled=True
                ).astype(jnp.float32),
                lax.psum_scatter(
                    shared_grad.astype(jnp.bfloat16), "tensor", scatter_dimension=0, tiled=True
                ).astype(jnp.float32),
            )
            shared_low = shared_local.astype(jnp.bfloat16)
            keyval_grad = jnp.einsum(
                "rd,rk->dk", normed_attn, shared_low, preferred_element_type=jnp.float32
            )
            attn_local = attn_local + jnp.einsum(
                "rk,dk->rd", shared_low, keyval_full, preferred_element_type=jnp.float32
            )
        _, norm_back = jax.vjp(normed_both, state, params)
        state_grad, param_grad = norm_back((attn_local, mlp_local))
        norm_grads[layer] = param_grad
        grad_state = grad_state + state_grad
    query_g, keyval_g, output_g, up_g, down_g, norm_g = (
        lax.psum_scatter(jnp.stack(query_grads), "dp", scatter_dimension=1, tiled=True),
        lax.psum_scatter(keyval_grad, "dp", scatter_dimension=0, tiled=True),
        lax.psum_scatter(jnp.stack(output_grads), "dp", scatter_dimension=2, tiled=True),
        lax.psum_scatter(jnp.stack(up_grads), "dp", scatter_dimension=1, tiled=True),
        lax.psum_scatter(jnp.stack(down_grads), "dp", scatter_dimension=2, tiled=True),
        lax.psum_scatter(jnp.stack(norm_grads), "dp", scatter_dimension=2, tiled=True),
    )
    keyval_g, norm_g = lax.psum((keyval_g, norm_g), "tensor")
    grads = (query_g, keyval_g, output_g, up_g, down_g, norm_g)
    firsts = (query_first, keyval_first, output_first, up_first, down_first, norm_first)
    seconds = (query_second, keyval_second, output_second, up_second, down_second, norm_second)
    parts = [
        lamb_parts(weight, first, second, grad)
        for weight, first, second, grad in zip(masters, firsts, seconds, grads)
    ]
    updates = tuple((part[2] for part in parts))
    update_local = param_squares(updates, leader)
    weight_total, update_total = lax.psum(
        (param_squares(masters, leader), update_local), ("dp", "tensor")
    )
    weight_norm = jnp.sqrt(weight_total)
    update_norms = jnp.sqrt(update_total)
    trust_ratios = weight_norm / update_norms
    query_next, keyval_next, output_next, up_next, down_next, norm_next = apply_trust(
        masters, updates, trust_ratios
    )
    return (
        current,
        grad_state,
        parts[0][0],
        parts[0][1],
        query_next,
        query_next.astype(jnp.bfloat16),
        parts[1][0],
        parts[1][1],
        keyval_next,
        keyval_next.astype(jnp.bfloat16),
        parts[2][0],
        parts[2][1],
        output_next,
        output_next.astype(jnp.bfloat16),
        parts[3][0],
        parts[3][1],
        up_next,
        up_next.astype(jnp.bfloat16),
        parts[4][0],
        parts[4][1],
        down_next,
        down_next.astype(jnp.bfloat16),
        parts[5][0],
        parts[5][1],
        norm_next,
        norm_next.astype(jnp.bfloat16),
        update_norms,
        trust_ratios,
    )


def solution(mesh):
    in_specs = (
        P(("dp", "tensor"), None),
        P(("dp", "tensor"), None),
        P("dp"),
        P(None, "dp", "tensor"),
        P("dp", None),
        P(None, "tensor", "dp"),
        P(None, "dp", "tensor"),
        P(None, "tensor", "dp"),
        P(None, None, "dp"),
        P(None, "dp", "tensor"),
        P(None, "dp", "tensor"),
        P("dp", None),
        P("dp", None),
        P(None, "tensor", "dp"),
        P(None, "tensor", "dp"),
        P(None, "dp", "tensor"),
        P(None, "dp", "tensor"),
        P(None, "tensor", "dp"),
        P(None, "tensor", "dp"),
        P(None, None, "dp"),
        P(None, None, "dp"),
    )
    out_specs = (
        P(("dp", "tensor"), None),
        P(("dp", "tensor"), None),
        P(None, "dp", "tensor"),
        P(None, "dp", "tensor"),
        P(None, "dp", "tensor"),
        P(None, "dp", "tensor"),
        P("dp", None),
        P("dp", None),
        P("dp", None),
        P("dp", None),
        P(None, "tensor", "dp"),
        P(None, "tensor", "dp"),
        P(None, "tensor", "dp"),
        P(None, "tensor", "dp"),
        P(None, "dp", "tensor"),
        P(None, "dp", "tensor"),
        P(None, "dp", "tensor"),
        P(None, "dp", "tensor"),
        P(None, "tensor", "dp"),
        P(None, "tensor", "dp"),
        P(None, "tensor", "dp"),
        P(None, "tensor", "dp"),
        P(None, None, "dp"),
        P(None, None, "dp"),
        P(None, None, "dp"),
        P(None, None, "dp"),
        P(),
        P(),
    )
    return jax.shard_map(shards, mesh=mesh, in_specs=in_specs, out_specs=out_specs, check_vma=False)
```

profile of v0, /device:TPU:0, one launch (start us, length us, event | category | flops | bytes accessed | tf_op | source)
XLA Modules:
  0.0 1750.0 jit_solution(9105149576013088518)
XLA Ops:
  11.1 32.7 %all_gather.40 = bf16[2,4,768]{1,0,2:T(2,128)(2,1)S(1)} all-gather(bf16[2,4,96]{1,0,2:T(2,128)(2,1)S(1)} %copy.149), channel_id=1, replica_groups=mesh['dp'=8,'tensor'=4] {'dp'}, dimensions={2}, use_global_device_ids=true | all-gather | bytes 13824 | tf_op jit(solution)/shard_map/all_gather | solution.py:233
  44.1 21.0 %slice_reduce_fusion.3 = (f32[768]{0:T(1024)}, f32[768]{0:T(1024)}, f32[768]{0:T(1024)}, f32[768]{0:T(1024)}, f32[768]{0:T(1024)S(1)}, /*index=5*/f32[768]{0:T(1024)S(1)}, f32[768]{0:T(1024)S(1)}, f32[768]{0:T(1024)S(1)}) fusion(f32[2,4,768]{1,0,2:T(2,128)S(1)} %convert_element_type.203), kind=kLoop, calls=%fused_computation.256 | loop fusion | bytes 49152 | tf_op jit(solution)/shard_map/slice | solution.py:245
  70.2 30.6 %all_gather.43 = bf16[768,128]{1,0:T(8,128)(2,1)S(1)} all-gather(bf16[96,128]{1,0:T(8,128)(2,1)S(1)} %convert_element_type.208), channel_id=1, replica_groups=mesh['dp'=8,'tensor'=4] {'dp'}, dimensions={0}, use_global_device_ids=true | all-gather | bytes 221184 | tf_op jit(solution)/shard_map/all_gather | solution.py:229
  100.8 32.9 %all_gather.44 = bf16[2,192,768]{1,0,2:T(2,128)(2,1)S(1)} all-gather(bf16[2,192,96]{1,0,2:T(2,128)(2,1)S(1)} %copy.152), channel_id=1, replica_groups=mesh['dp'=8,'tensor'=4] {'dp'}, dimensions={2}, use_global_device_ids=true | all-gather | bytes 663552 | tf_op jit(solution)/shard_map/all_gather | solution.py:230
  133.7 34.4 %all_gather.42 = bf16[2,768,192]{2,1,0:T(8,128)(2,1)S(1)} all-gather(bf16[2,96,192]{2,1,0:T(8,128)(2,1)S(1)} %get-tuple-element.629), channel_id=1, replica_groups=mesh['dp'=8,'tensor'=4] {'dp'}, dimensions={1}, use_global_device_ids=true | all-gather | bytes 663552 | tf_op jit(solution)/shard_map/all_gather | solution.py:228
  180.0 97.5 %while.58 = (s32[]{:T(128)}, bf16[4,512,3,64]{1,3,2,0:T(8,128)(2,1)S(1)}, f32[4,3,512,1]{2,1,3,0:T(4,128)S(1)}, s32[4]{0:T(128)S(1)}, bf16[2048,3,64]{0,2,1:T(8,...) while((s32[]{:T(128)}, ...), condition=%wide.region_5.6_spmd, body=%wide.region_2.5_spmd.sunk | while | flops 844200960 | bytes 42924204 | solution.py:107
  278.9 29.9 %multiply_convert_fusion.1 = (bf16[2048,768]{1,0:T(8,128)(2,1)}, f32[2048,768]{1,0:T(8,128)}, f32[2048,768]{1,0:T(8,128)}) fusion(bf16[2048,768]{1,0:T(8,128)(2,1)} %all-gather.11.cloned.1.call-done, bf16[2,768,768]{2,1,0:T(8,128)(2,1)} %all-gather.13.cloned.1.call-done), kind=kOutput, calls=%fused_computation.129 | convolution fusion | flops 2518155264 | bytes 20054016 | tf_op jit(solution)/shard_map/dot_general | solution.py:255
  320.0 57.2 %reduce-scatter.19.cloned.1.call-done = f32[512,768]{1,0:T(8,128)} async-done(((f32[2048,768]{1,0:T(8,128)}), f32[512,768]{1,0:T(8,128)}) %reduce-scatter.19.cloned.1.call-update) | async-done | bytes 1572880 | tf_op jit(solution)/shard_map/reduce_scatter | solution.py:262
  382.5 24.9 %all-gather.21.cloned.1.call-done = bf16[2048,768]{1,0:T(8,128)(2,1)} async-done(((bf16[512,768]{1,0:T(8,128)(2,1)}), bf16[2048,768]{1,0:T(8,128)(2,1)}) %all-gather.21.cloned.1.call-update) | async-done | bytes 3145744 | tf_op jit(solution)/shard_map/all_gather | solution.py:275
  410.5 27.0 %all-gather.17.cloned.1.call-done = bf16[2048,768]{1,0:T(8,128)(2,1)} async-done(((bf16[512,768]{1,0:T(8,128)(2,1)}), bf16[2048,768]{1,0:T(8,128)(2,1)}) %all-gather.17.cloned.1.call-update) | async-done | bytes 3145744 | tf_op jit(solution)/shard_map/all_gather | solution.py:39
  441.9 97.3 %while.59 = (s32[]{:T(128)}, bf16[4,512,3,64]{1,3,2,0:T(8,128)(2,1)S(1)}, f32[4,3,512,1]{2,1,3,0:T(4,128)S(1)}, s32[4]{0:T(128)S(1)}, bf16[2048,3,64]{0,2,1:T(8,...) while((s32[]{:T(128)}, ...), condition=%wide.region_12.13_spmd, body=%wide.region_9.12_spmd.sunk | while | flops 844200960 | bytes 42924204 | solution.py:107
  541.7 152.0 %while.60 = (s32[]{:T(128)}, f32[2048,64]{0,1:T(8,128)S(1)}, f32[2048,64]{0,1:T(8,128)S(1)}, bf16[4,512,3,64]{1,3,2,0:T(8,128)(2,1)}, f32[4,512,3,64]{1,0,3,2:T(...) while((s32[]{:T(128)}, f32[2048,64]{0,1:T(8,128)S(1)}, ...), condition=%wide.region_19.20_spmd.clone, body=%wide.region_17.19_spmd.clone.sunk | while | flops 2477587456 | bytes 129030624 | solution.py:148
  571.3 8.6 dynamic_update_slice.50
  609.1 8.6 dynamic_update_slice.50
  647.0 8.6 dynamic_update_slice.50
  684.9 8.6 dynamic_update_slice.50
  701.1 17.9 %multiply_convert_fusion = (bf16[2048,768]{1,0:T(8,128)(2,1)}, f32[2048,768]{1,0:T(8,128)S(1)}, f32[2048,768]{1,0:T(8,128)S(1)}) fusion(bf16[2048,768]{1,0:T(8,128)(2,1)} %all-gather.19.cloned.1.call-done, bf16[2,768,768]{2,1,0:T(8,128)(2,1)} %all-gather.13.cloned.1.call-done), kind=kOutput, calls=%fused_computation.116 | convolution fusion | flops 2518155264 | bytes 20054016 | tf_op jit(solution)/shard_map/dot_general | solution.py:255
  739.1 40.4 %reduce-scatter.23.cloned.1.call-done = bf16[512,768]{1,0:T(8,128)(2,1)} async-done(((bf16[2048,768]{1,0:T(8,128)(2,1)}), bf16[512,768]{1,0:T(8,128)(2,1)}) %reduce-scatter.23.cloned.1.call-update) | async-done | bytes 786448 | tf_op jit(solution)/shard_map/reduce_scatter | solution.py:323
  785.8 54.8 %reduce-scatter.21.cloned.1.call-done = f32[512,768]{1,0:T(8,128)} async-done(((f32[2048,768]{1,0:T(8,128)}), f32[512,768]{1,0:T(8,128)}) %reduce-scatter.21.cloned.1.call-update) | async-done | bytes 1572880 | tf_op jit(solution)/shard_map/reduce_scatter | solution.py:262
  844.8 28.6 %all-gather.23.cloned.1.call-done = bf16[2048,768]{1,0:T(8,128)(2,1)} async-done(((bf16[512,768]{1,0:T(8,128)(2,1)}), bf16[2048,768]{1,0:T(8,128)(2,1)}) %all-gather.23.cloned.1.call-update) | async-done | bytes 3145744 | tf_op jit(solution)/shard_map/all_gather | solution.py:275
  879.7 157.9 %while.61 = (s32[]{:T(128)}, f32[2048,64]{0,1:T(8,128)}, f32[2048,64]{0,1:T(8,128)}, bf16[4,512,3,64]{1,3,2,0:T(8,128)(2,1)}, f32[4,512,3,64]{1,0,3,2:T(4,128)},...) while((s32[]{:T(128)}, f32[2048,64]{0,1:T(8,128)}, ...), condition=%wide.region_28.29_spmd.clone, body=%wide.region_26.28_spmd.clone.sunk | while | flops 2477587456 | bytes 122540376 | solution.py:148
  950.1 8.6 dynamic_update_slice.52
  1041.5 9.2 add_convert_fusion
  1110.3 33.9 %reduce-scatter.29.cloned.1.call-done = bf16[512,768]{1,0:T(8,128)(2,1)} async-done(((bf16[2048,768]{1,0:T(8,128)(2,1)}), bf16[512,768]{1,0:T(8,128)(2,1)}) %reduce-scatter.29.cloned.1.call-update) | async-done | bytes 786448 | tf_op jit(solution)/shard_map/reduce_scatter | solution.py:329
  1163.9 48.1 %reduce-scatter.37.cloned.1.call-done = f32[96,384]{1,0:T(8,128)} async-done(((f32[768,384]{1,0:T(8,128)}), f32[96,384]{1,0:T(8,128)}) %reduce-scatter.37.cloned.1.call-update) | async-done | bytes 147472
  1216.1 62.7 %reduce-scatter.39.cloned.1.call-done = f32[96,384]{1,0:T(8,128)} async-done(((f32[768,384]{1,0:T(8,128)}), f32[96,384]{1,0:T(8,128)}) %reduce-scatter.39.cloned.1.call-update) | async-done | bytes 147472
  1282.5 168.8 %all-reduce.13.cloned.1.call-done = f32[2,768,768]{1,0,2:T(2,128)} async-done(((f32[2,768,768]{1,0,2:T(2,128)}), f32[2,768,768]{1,0,2:T(2,128)}) %all-reduce.13.cloned.1.call-update) | async-done | bytes 4718608
  1458.6 57.4 %reduce-scatter.41.cloned.1.call-done = f32[96,8]{1,0:T(8,128)} async-done(((f32[768,8]{1,0:T(8,128)}), f32[96,8]{1,0:T(8,128)}) %reduce-scatter.41.cloned.1.call-update) | async-done | bytes 3088
  1519.1 61.4 %reduce-scatter.33.cloned.1.call-done = f32[96,128]{1,0:T(8,128)} async-done(((f32[768,128]{1,0:T(8,128)}), f32[96,128]{1,0:T(8,128)}) %reduce-scatter.33.cloned.1.call-update) | async-done | bytes 49168 | tf_op jit(solution)/shard_map/reduce_scatter | solution.py:352
  1580.5 12.0 all-reduce.10
  1602.3 76.8 %reduce-scatter.35.cloned.1.call-done = f32[2,96,768]{2,1,0:T(8,128)} async-done(((f32[2,768,768]{2,1,0:T(8,128)}), f32[2,96,768]{2,1,0:T(8,128)}) %reduce-scatter.35.cloned.1.call-update) | async-done | bytes 589840 | tf_op jit(solution)/shard_map/reduce_scatter | solution.py:354
  1688.7 40.5 %all-reduce.9 = (f32[17]{0:T(128)S(1)}, f32[17]{0:T(128)S(1)}) all-reduce(f32[17]{0:T(128)} %concatenate.42, f32[17]{0:T(128)} %concatenate.41), channel_id=1, replica_groups=mesh['dp'=8,'tensor'=4] {'dp','tensor'}, use_global_device_ids=true, to_apply=%region_62.63 | all-reduce | flops 34 | bytes 272 | tf_op jit(solution)/shard_map/psum | solution.py:368
  (645 shorter events, 645.9 us)
Async XLA Ops:
  7.2 166.7 %all-gather.9.cloned.1.call-start = ((), (), s32[]{:S(2)}) async-start(), calls=%async_computation.12 | async-start | bytes 3932160 | tf_op jit(solution)/shard_map/all_gather | solution.py:39
  66.8 212.1 %all-gather.13.cloned.1.call-start = ((), (), s32[]{:S(2)}) async-start(), calls=%async_computation.14 | async-start | bytes 2654208 | tf_op jit(solution)/shard_map/all_gather | solution.py:231
  67.6 211.3 %all-gather.11.cloned.1.call-start = ((), (), s32[]{:S(2)}) async-start(), calls=%async_computation.13 | async-start | bytes 3932160 | tf_op jit(solution)/shard_map/all_gather | solution.py:40
  68.4 240.5 %all-gather.15.cloned.1.call-start = ((), (), s32[]{:S(2)}) async-start(), calls=%async_computation.15 | async-start | bytes 2654208 | tf_op jit(solution)/shard_map/all_gather | solution.py:232
  69.2 308.1 %reduce-scatter.19.cloned.1.call-start = ((), (), s32[]{:S(2)}) async-start(), calls=%async_computation.16 | async-start | bytes 7864320 | tf_op jit(solution)/shard_map/reduce_scatter | solution.py:262
  317.6 89.7 %all-gather.21.cloned.1.call-start = ((), (), s32[]{:S(2)}) async-start(), calls=%async_computation.20 | async-start | bytes 3932160 | tf_op jit(solution)/shard_map/all_gather | solution.py:275
  320.0 117.6 %all-gather.17.cloned.1.call-start = ((), (), s32[]{:S(2)}) async-start(), calls=%async_computation.17 | async-start | bytes 3932160 | tf_op jit(solution)/shard_map/all_gather | solution.py:39
  381.7 319.3 %all-gather.19.cloned.1.call-start = ((), (), s32[]{:S(2)}) async-start(), calls=%async_computation.18 | async-start | bytes 3932160 | tf_op jit(solution)/shard_map/all_gather | solution.py:40
  410.5 328.7 %reduce-scatter.25.cloned.1.call-start = ((), (), s32[]{:S(2)}) async-start(), calls=%async_computation.22 | async-start | bytes 3932160 | tf_op jit(solution)/shard_map/reduce_scatter | solution.py:320
  541.6 155.5 %copy-start.40 = (f32[2048,8]{0,1:T(8,128)S(1)}, f32[2048,8]{0,1:T(8,128)}, u32[]{:S(2)}) copy-start(f32[2048,8]{0,1:T(8,128)} %copy-done.38) | copy-start | bytes 196612
  701.0 78.5 %reduce-scatter.23.cloned.1.call-start = ((), (), s32[]{:S(2)}) async-start(), calls=%async_computation.21 | async-start | bytes 3932160 | tf_op jit(solution)/shard_map/reduce_scatter | solution.py:323
  729.0 111.7 %reduce-scatter.21.cloned.1.call-start = ((), (), s32[]{:S(2)}) async-start(), calls=%async_computation.19 | async-start | bytes 7864320 | tf_op jit(solution)/shard_map/reduce_scatter | solution.py:262
  738.9 134.6 %all-gather.23.cloned.1.call-start = ((), (), s32[]{:S(2)}) async-start(), calls=%async_computation.23 | async-start | bytes 3932160 | tf_op jit(solution)/shard_map/all_gather | solution.py:275
  844.7 265.5 %reduce-scatter.31.cloned.1.call-start = ((), (), s32[]{:S(2)}) async-start(), calls=%async_computation.26 | async-start | bytes 655360 | tf_op jit(solution)/shard_map/reduce_scatter | solution.py:335
  879.7 157.9 %copy-start.6 = (f32[2048,64]{0,1:T(8,128)S(1)}, f32[2048,64]{0,1:T(8,128)}, u32[]{:S(2)}) copy-start(f32[2048,64]{0,1:T(8,128)} %copy-done.5) | copy-start | bytes 1572868
  879.7 159.2 %copy-start.69 = (f32[2048]{0:T(1024)S(1)}, f32[2048]{0:T(1024)}, u32[]{:S(2)}) copy-start(f32[2048]{0:T(1024)} %copy-done.68) | copy-start | bytes 24580
  879.7 159.2 %copy-start.102 = (f32[8]{0:T(128)S(1)}, f32[8]{0:T(128)}, u32[]{:S(2)}) copy-start(f32[8]{0:T(128)} %copy-done.101) | copy-start | bytes 100
  1041.5 68.8 %reduce-scatter.27.cloned.1.call-start = ((), (), s32[]{:S(2)}) async-start(), calls=%async_computation.24 | async-start | bytes 3932160 | tf_op jit(solution)/shard_map/reduce_scatter | solution.py:332
  1056.4 87.8 %reduce-scatter.29.cloned.1.call-start = ((), (), s32[]{:S(2)}) async-start(), calls=%async_computation.25 | async-start | bytes 3932160 | tf_op jit(solution)/shard_map/reduce_scatter | solution.py:329
  1064.9 147.0 %reduce-scatter.37.cloned.1.call-start = ((), (), s32[]{:S(2)}) async-start(), calls=%async_computation.29 | async-start | bytes 1327104
  1072.2 206.6 %reduce-scatter.39.cloned.1.call-start = ((), (), s32[]{:S(2)}) async-start(), calls=%async_computation.30 | async-start | bytes 1327104
  1083.4 367.9 %all-reduce.13.cloned.1.call-start = ((), (), s32[]{:S(2)}) async-start(), calls=%async_computation.32 | async-start | bytes 9437184
  1102.8 413.2 %reduce-scatter.41.cloned.1.call-start = ((), (), s32[]{:S(2)}) async-start(), calls=%async_computation.31 | async-start | bytes 442368
  1151.6 428.9 %reduce-scatter.33.cloned.1.call-start = ((), (), s32[]{:S(2)}) async-start(), calls=%async_computation.27 | async-start | bytes 442368 | tf_op jit(solution)/shard_map/reduce_scatter | solution.py:352
  1152.9 526.2 %reduce-scatter.35.cloned.1.call-start = ((), (), s32[]{:S(2)}) async-start(), calls=%async_computation.28 | async-start | bytes 5308416 | tf_op jit(solution)/shard_map/reduce_scatter | solution.py:354
  1161.3 118.8 %copy-start.36 = (f32[2,192,96]{2,1,0:T(8,128)S(1)}, f32[2,192,96]{2,1,0:T(8,128)}, u32[]{:S(2)}) copy-start(f32[2,192,96]{2,1,0:T(8,128)} %param.34) | copy-start | bytes 442372
  1161.3 118.8 %copy-start.61 = (f32[2,192,96]{2,1,0:T(8,128)S(1)}, f32[2,192,96]{2,1,0:T(8,128)}, u32[]{:S(2)}) copy-start(f32[2,192,96]{2,1,0:T(8,128)} %param.42) | copy-start | bytes 442372
  1161.3 291.2 %copy-start.24 = (f32[2,768,96]{1,2,0:T(8,128)S(1)}, f32[2,768,96]{1,2,0:T(8,128)}, u32[]{:S(2)}) copy-start(f32[2,768,96]{1,2,0:T(8,128)} %param.36) | copy-start | bytes 1769476
  1162.3 289.0 %copy-start.37 = (f32[2,96,192]{1,2,0:T(8,128)}, f32[2,96,192]{1,2,0:T(8,128)S(1)}, u32[]{:S(2)}) copy-start(f32[2,96,192]{1,2,0:T(8,128)S(1)} %copy.168) | copy-start | bytes 442372
  1213.1 379.4 %copy-start.82 = (f32[2,4,96]{2,1,0:T(4,128)S(1)}, f32[2,4,96]{2,1,0:T(4,128)}, u32[]{:S(2)}) copy-start(f32[2,4,96]{2,1,0:T(4,128)} %param.37) | copy-start | bytes 9220
  1214.5 464.6 %copy-start.26 = (f32[2,96,768]{2,1,0:T(8,128)S(1)}, f32[2,96,768]{2,1,0:T(8,128)}, u32[]{:S(2)}) copy-start(f32[2,96,768]{2,1,0:T(8,128)} %param.35) | copy-start | bytes 1769476
  1452.5 232.9 %copy-start.20 = (f32[512,768]{1,0:T(8,128)S(1)}, f32[512,768]{1,0:T(8,128)}, u32[]{:S(2)}) copy-start(f32[512,768]{1,0:T(8,128)} %get-tuple-element.584) | copy-start | bytes 4718596
  (124 other events, 2629.9 us)
Sparse Core Ops, SparseCore 0:
  66.9 29.5 all-gather.8
  99.3 62.2 all-gather.12
  163.8 28.4 all-gather.10
  194.9 52.0 all-gather.14
  317.7 59.5 reduce-scatter.18
  378.8 28.5 all-gather.20
  409.0 28.5 all-gather.16
  439.2 28.5 all-gather.18
  701.1 37.9 reduce-scatter.24
  741.5 37.9 reduce-scatter.22
  782.2 58.3 reduce-scatter.20
  844.8 28.5 all-gather.22
  1041.6 21.6 reduce-scatter.30
  1065.8 37.9 reduce-scatter.26
  1106.2 37.9 reduce-scatter.28
  1147.8 64.0 reduce-scatter.36
  1215.5 63.2 reduce-scatter.38
  1282.7 168.5 all-reduce.12
  1455.5 60.4 reduce-scatter.40
  1520.1 60.3 reduce-scatter.32
  1584.6 94.4 reduce-scatter.34
where the time goes:
time: 1760 us; the launch traced here: 1750 us
  waiting for transfers between devices  743 us (42%)
  matrix products  417 us (24%)
  blocking collectives  183 us (10%)
  local copies, waits for them, and re-layouts  175 us (10%)
  other arithmetic  172 us (10%)
  loops' own time  38.6 us (2%)
  between operations  19.2 us (1%)
    unnamed x25, waiting for transfers between devices  338 us
    reduce_scatter x2, waiting for transfers between devices, shards(): lax.psum_scatter(term, 'tensor', scatter_dimension=0, tiled=True)  112 us
    dot_general x16, matrix products, masked_scores(): jnp.einsum('qhd,kd->hqk', query_block, keys, preferred_element_type=jnp.f...  77.6 us
    reduce_scatter x1, waiting for transfers between devices, shards(): lax.psum_scatter(jnp.stack(up_grads), 'dp', scatter_dimension=1, tiled=True)  76.8 us
    dynamic_update_slice x16, local copies, waits for them, and re-layouts, attention_backward(): lax.scan(one, (empty, empty), jnp.arange(length // block))  72.1 us
    reduce_scatter x1, waiting for transfers between devices, shards(): lax.psum_scatter(keyval_grad, 'dp', scatter_dimension=0, tiled=True)  61.4 us
    reduce_sum x8, other arithmetic, one(): total = jnp.sum(weights, axis=-1, keepdims=True)  54.2 us
    dot_general x8, matrix products, one(): jnp.einsum('hqk,kd->qhd', probs, values, preferred_element_type=jnp.float32)  53.9 us
  transfers between devices with their start and end apart: 21, of which 14 were waited for; matrix products, arithmetic and copies ran while one was open for 30% of the time, Pallas kernels for 0%

commit v1 on v0

v1 whole, which is shorter than its diff:
```python
import functools
import math

import jax
import jax.numpy as jnp
from jax import lax
from jax.experimental import pallas as pl
from jax.experimental.pallas import tpu as pltpu
from jax.sharding import PartitionSpec as P

F32 = jnp.float32
BF16 = jnp.bfloat16
MESH = pl.DeviceIdType.MESH

HD = 64
ROT = 16
HALF = ROT // 2
STEP = 5
HEADS_HERE = 3
QW = 192

NORM_EPSILON = 1e-05
BETA_FIRST = 0.5
BETA_SECOND = 0.55
ADAM_EPSILON = 1e-06
WEIGHT_DECAY = 0.01
LEARN_RATE = 0.5
SCALE = HD**-0.5
MIB = 2**20


def dot(a, b):
    return jnp.dot(a, b, preferred_element_type=F32)


def dot_nt(a, b):
    return lax.dot_general(a, b, (((1,), (1,)), ((), ())), preferred_element_type=F32)


def turn(a):
    return jnp.transpose(a.astype(F32), (1, 0))


def standard(values):
    center = values - jnp.mean(values, axis=-1, keepdims=True)
    spread = jnp.mean(center * center, axis=-1, keepdims=True)
    inverse = lax.rsqrt(spread + NORM_EPSILON)
    return center * inverse, inverse


def gelu_parts(v):
    x = jnp.abs(v) * (2.0**-0.5)
    bell = jnp.exp(-x * x)
    t = 1.0 / (1.0 + 0.3275911 * x)
    series = t * (
        0.254829592
        + t * (-0.284496736 + t * (1.421413741 + t * (-1.453152027 + t * 1.061405429)))
    )
    tail = 0.5 * series * bell
    cumulative = jnp.where(v < 0.0, tail, 1.0 - tail)
    return cumulative, bell * (1.0 / math.sqrt(2.0 * math.pi))


def rotated(low, cos, sin):
    first, second = low[:HALF], low[HALF:ROT]
    return jnp.concatenate([first * cos - second * sin, second * cos + first * sin], axis=0)


def qkv_kernel(first, x_ref, norm_ref, trig_ref, qk_ref, *rest):
    if first:
        ov_ref, qt_ref, kv_ref, normed = rest
    else:
        qt_ref, normed = rest
    t = pl.program_id(0)

    @pl.when(t == 0)
    def _():
        x = x_ref[...].astype(F32)
        normed[...] = (standard(x)[0] * norm_ref[0:1] + norm_ref[1:2]).astype(BF16)

    cos, sin = trig_ref[0:HALF], trig_ref[HALF:ROT]
    lin = turn(dot(normed[...], qk_ref[0]))
    for head in range(HEADS_HERE):
        base = head * HD
        low = rotated(lin[base : base + ROT], cos, sin)
        qt_ref[0, base : base + ROT] = (low.astype(BF16).astype(F32) * SCALE).astype(BF16)
        qt_ref[0, base + ROT : base + HD] = (
            lin[base + ROT : base + HD].astype(BF16).astype(F32) * SCALE
        ).astype(BF16)
    qt_ref[0, QW:] = jnp.zeros_like(qt_ref[0, QW:])
    if first:

        @pl.when(t == 0)
        def _():
            value = turn(dot(normed[...], ov_ref[0]))[QW:]
            key = jnp.concatenate(
                [rotated(lin[QW : QW + ROT], cos, sin), lin[QW + ROT :]], axis=0
            )
            kv_ref[...] = turn(jnp.concatenate([key, value], axis=0)).astype(BF16)


def qkv_call(first, x, norms, trig, weights):
    rows, width = x.shape
    tens = weights.shape[0]
    whole = pl.BlockSpec(memory_space=pltpu.VMEM)
    in_specs = [whole, whole, whole, pl.BlockSpec((1, width, 256), lambda t: (t, 0, 6))]
    out_shape = [jax.ShapeDtypeStruct((tens, 256, rows), BF16)]
    out_specs = [pl.BlockSpec((1, 256, rows), lambda t: (t, 0, 0))]
    args = [x, norms, trig, weights]
    if first:
        in_specs.append(pl.BlockSpec((1, width, 256), lambda t: (0, 0, 7)))
        args.append(weights)
        out_shape.append(jax.ShapeDtypeStruct((rows, 2 * HD), BF16))
        out_specs.append(whole)
    return pl.pallas_call(
        functools.partial(qkv_kernel, first),
        grid=(tens,),
        in_specs=in_specs,
        out_specs=out_specs,
        out_shape=out_shape,
        scratch_shapes=[pltpu.VMEM((rows, width), BF16)],
        compiler_params=pltpu.CompilerParams(vmem_limit_bytes=32 * MIB),
    )(*args)


def attend_kernel(qt_ref, kv_ref, at_ref, lse_ref, keys, values_t):
    t = pl.program_id(0)
    rows = qt_ref.shape[2]
    place = lax.axis_index("tensor")

    @pl.when(t == 0)
    def _():
        keys[...] = kv_ref[:, :HD]
        values_t[...] = turn(kv_ref[...])[HD:].astype(BF16)

    def block(index, carry, diagonal):
        key = keys[pl.ds(pl.multiple_of(index * rows, rows), rows), :]
        value_t = values_t[:, pl.ds(pl.multiple_of(index * rows, rows), rows)]
        out = []
        for head in range(HEADS_HERE):
            scores = dot(key, qt_ref[0, head * HD : (head + 1) * HD])
            if diagonal:
                below = lax.broadcasted_iota(jnp.int32, scores.shape, 0)
                across = lax.broadcasted_iota(jnp.int32, scores.shape, 1)
                scores = jnp.where(below <= across, scores, -1e30)
            peak = jnp.max(scores, axis=0, keepdims=True)
            if carry is not None:
                peak = jnp.maximum(peak, carry[head][0])
            weights = jnp.exp(scores - peak)
            total = jnp.sum(weights, axis=0, keepdims=True)
            mixed = dot(value_t, weights.astype(BF16))
            if carry is not None:
                fade = jnp.exp(carry[head][0] - peak)
                total = total + carry[head][1] * fade
                mixed = mixed + carry[head][2] * fade
            out.append((peak, total, mixed))
        return tuple(out)

    carry = block(place, None, True)
    carry = lax.fori_loop(0, place, lambda i, c: block(i, c, False), carry)
    lse_ref[...] = jnp.zeros_like(lse_ref)
    for head in range(HEADS_HERE):
        peak, total, mixed = carry[head]
        at_ref[0, head * HD : (head + 1) * HD] = (mixed / total).astype(BF16)
        lse_ref[0, head : head + 1] = peak + jnp.log(total)
    at_ref[0, QW:] = jnp.zeros_like(at_ref[0, QW:])


def attend_call(qt, kv):
    tens, _, rows = qt.shape
    length = kv.shape[0]
    whole = pl.BlockSpec(memory_space=pltpu.VMEM)
    part = pl.BlockSpec((1, 256, rows), lambda t: (t, 0, 0))
    return pl.pallas_call(
        attend_kernel,
        grid=(tens,),
        in_specs=[part, whole],
        out_specs=[part, pl.BlockSpec((1, 8, rows), lambda t: (t, 0, 0))],
        out_shape=[
            jax.ShapeDtypeStruct((tens, 256, rows), BF16),
            jax.ShapeDtypeStruct((tens, 8, rows), F32),
        ],
        scratch_shapes=[pltpu.VMEM((length, HD), BF16), pltpu.VMEM((HD, length), BF16)],
        compiler_params=pltpu.CompilerParams(vmem_limit_bytes=48 * MIB),
    )(qt, kv)


def mix_kernel(x_ref, norm_ref, at_ref, o_ref, up_ref, down_ref, out_ref, act_ref, slope_ref, normed, total):
    t = pl.program_id(0)

    @pl.when(t == 0)
    def _():
        x = x_ref[...].astype(F32)
        normed[...] = (standard(x)[0] * norm_ref[2:3] + norm_ref[3:4]).astype(BF16)
        total[...] = x

    attended = turn(at_ref[0, :QW]).astype(BF16)
    step = 256
    for start in range(0, up_ref.shape[2], step):
        cols = pl.ds(start, step)
        pre = dot(normed[...], up_ref[0, :, cols])
        cumulative, bell = gelu_parts(pre)
        act_ref[0, :, cols] = (pre * cumulative).astype(BF16)
        slope_ref[0, :, cols] = (cumulative + pre * bell).astype(BF16)
    total[...] += dot_nt(attended, o_ref[0, :, :QW]) + dot_nt(act_ref[0], down_ref[0])

    @pl.when(t == pl.num_programs(0) - 1)
    def _():
        out_ref[...] = total[...]


def mix_call(x, norms, at, weights):
    rows, width = x.shape
    tens = weights.shape[0]
    hidden = 768
    whole = pl.BlockSpec(memory_space=pltpu.VMEM)
    wide = pl.BlockSpec((1, rows, hidden), lambda t: (t, 0, 0))
    return pl.pallas_call(
        mix_kernel,
        grid=(tens,),
        in_specs=[
            whole,
            whole,
            pl.BlockSpec((1, 256, rows), lambda t: (t, 0, 0)),
            pl.BlockSpec((1, width, 256), lambda t: (t, 0, 7)),
            pl.BlockSpec((1, width, hidden), lambda t: (t, 0, 0)),
            pl.BlockSpec((1, width, hidden), lambda t: (t, 0, 1)),
        ],
        out_specs=[whole, wide, wide],
        out_shape=[
            jax.ShapeDtypeStruct((rows, width), F32),
            jax.ShapeDtypeStruct((tens, rows, hidden), BF16),
            jax.ShapeDtypeStruct((tens, rows, hidden), BF16),
        ],
        scratch_shapes=[pltpu.VMEM((rows, width), BF16), pltpu.VMEM((rows, width), F32)],
        compiler_params=pltpu.CompilerParams(vmem_limit_bytes=48 * MIB),
    )(x, norms, at, weights, weights, weights)


def mix_back_kernel(
    gx_ref, x_ref, norm_ref, at_ref, act_ref, slope_ref, o_ref, up_ref, down_ref,
    pack_ref, dot_ref, mlp_ref, low, low_t, normed_t,
):
    t = pl.program_id(0)

    @pl.when(t == 0)
    def _():
        grad = gx_ref[...].astype(BF16)
        low[...] = grad
        low_t[...] = turn(grad).astype(BF16)
        x = x_ref[...].astype(F32)
        normed = (standard(x)[0] * norm_ref[2:3] + norm_ref[3:4]).astype(BF16)
        normed_t[...] = turn(normed).astype(BF16)
        mlp_ref[...] = jnp.zeros_like(mlp_ref)

    hidden = up_ref.shape[2]
    grad_attended = dot(low[...], o_ref[0, :, :QW])
    dot_ref[0, :QW] = turn(grad_attended).astype(BF16)
    dot_ref[0, QW:] = jnp.zeros_like(dot_ref[0, QW:])
    pack_ref[0, :, 2 * hidden :] = dot_nt(low_t[...], at_ref[0]).astype(BF16)
    pack_ref[0, :, hidden : 2 * hidden] = dot(low_t[...], act_ref[0]).astype(BF16)
    grad_pre = (dot(low[...], down_ref[0]) * slope_ref[0].astype(F32)).astype(BF16)
    pack_ref[0, :, :hidden] = dot(normed_t[...], grad_pre).astype(BF16)
    mlp_ref[...] += dot_nt(grad_pre, up_ref[0])


def mix_back_call(gx, x, norms, at, act, slope, weights):
    rows, width = x.shape
    tens = weights.shape[0]
    hidden = act.shape[2]
    whole = pl.BlockSpec(memory_space=pltpu.VMEM)
    wide = pl.BlockSpec((1, rows, hidden), lambda t: (t, 0, 0))
    part = pl.BlockSpec((1, 256, rows), lambda t: (t, 0, 0))
    return pl.pallas_call(
        mix_back_kernel,
        grid=(tens,),
        in_specs=[
            whole,
            whole,
            whole,
            part,
            wide,
            wide,
            pl.BlockSpec((1, width, 256), lambda t: (t, 0, 7)),
            pl.BlockSpec((1, width, hidden), lambda t: (t, 0, 0)),
            pl.BlockSpec((1, width, hidden), lambda t: (t, 0, 1)),
        ],
        out_specs=[
            pl.BlockSpec((1, width, 2 * hidden + 256), lambda t: (t, 0, 0)),
            part,
            whole,
        ],
        out_shape=[
            jax.ShapeDtypeStruct((tens, width, 2 * hidden + 256), BF16),
            jax.ShapeDtypeStruct((tens, 256, rows), BF16),
            jax.ShapeDtypeStruct((rows, width), F32),
        ],
        scratch_shapes=[
            pltpu.VMEM((rows, width), BF16),
            pltpu.VMEM((width, rows), BF16),
            pltpu.VMEM((width, rows), BF16),
        ],
        compiler_params=pltpu.CompilerParams(vmem_limit_bytes=56 * MIB),
    )(gx, x, norms, at, act, slope, weights, weights, weights)


def attend_back_kernel(
    start_given, qt_ref, dot_ref, at_ref, lse_ref, kv_ref, trig_ref, *rest
):
    if start_given:
        before_ref, gqt_ref, dkv_ref, keys, values, keys_t, dkeys, dvalues = rest
    else:
        gqt_ref, dkv_ref, keys, values, keys_t, dkeys, dvalues = rest
    t = pl.program_id(0)
    rows = qt_ref.shape[2]
    place = lax.axis_index("tensor")

    @pl.when(t == 0)
    def _():
        both_t = turn(kv_ref[...])
        keys[...] = kv_ref[:, :HD]
        keys_t[...] = both_t[:HD].astype(BF16)
        values[...] = turn(both_t[HD:]).astype(BF16)
        dkeys[...] = jnp.zeros_like(dkeys)
        dvalues[...] = jnp.zeros_like(dvalues)

    inner = []
    for head in range(HEADS_HERE):
        span = slice(head * HD, (head + 1) * HD)
        inner.append(
            jnp.sum(
                dot_ref[0, span].astype(F32) * at_ref[0, span].astype(F32), axis=0, keepdims=True
            )
        )

    def block(index, carry, diagonal):
        here = pl.ds(pl.multiple_of(index * rows, rows), rows)
        key = keys[here, :]
        value = values[here, :]
        key_t = keys_t[:, here]
        out = []
        dkey = None
        for head in range(HEADS_HERE):
            span = slice(head * HD, (head + 1) * HD)
            query_t = qt_ref[0, span]
            grad_t = dot_ref[0, span]
            scores = dot(key, query_t)
            probs = jnp.exp(scores - lse_ref[0, head : head + 1])
            if diagonal:
                below = lax.broadcasted_iota(jnp.int32, scores.shape, 0)
                across = lax.broadcasted_iota(jnp.int32, scores.shape, 1)
                probs = jnp.where(below <= across, probs, 0.0)
            grad_probs = dot(value, grad_t)
            grad_scores = (probs * (grad_probs - inner[head])).astype(BF16)
            part_v = dot_nt(probs.astype(BF16), grad_t)
            part_k = dot_nt(grad_scores, query_t)
            dkey = part_k if dkey is None else dkey + part_k
            dvalue = part_v if head == 0 else dvalue + part_v
            part_q = dot(key_t, grad_scores)
            out.append(part_q if carry is None else carry[head] + part_q)
        dkeys[here, :] += dkey
        dvalues[here, :] += dvalue
        return tuple(out)

    carry = block(place, None, True)
    carry = lax.fori_loop(0, place, lambda i, c: block(i, c, False), carry)
    cos, sin = trig_ref[0:HALF], trig_ref[HALF:ROT]
    for head in range(HEADS_HERE):
        base = head * HD
        grad = carry[head] * SCALE
        gqt_ref[0, base : base + ROT] = rotated(grad[:ROT], cos, -sin).astype(BF16)
        gqt_ref[0, base + ROT : base + HD] = grad[ROT:].astype(BF16)
    gqt_ref[0, QW:] = jnp.zeros_like(gqt_ref[0, QW:])

    @pl.when(t == pl.num_programs(0) - 1)
    def _():
        both = jnp.concatenate([turn(dkeys[...]), turn(dvalues[...])], axis=0)
        for part in range(dkv_ref.shape[0]):
            piece = both[:, part * rows : (part + 1) * rows]
            if start_given:
                piece = piece + before_ref[part]
            dkv_ref[part] = piece


def attend_back_call(qt, dout, at, lse, kv, trig, before=None):
    tens, _, rows = qt.shape
    length = kv.shape[0]
    whole = pl.BlockSpec(memory_space=pltpu.VMEM)
    part = pl.BlockSpec((1, 256, rows), lambda t: (t, 0, 0))
    args = [qt, dout, at, lse, kv, trig]
    in_specs = [part, part, part, pl.BlockSpec((1, 8, rows), lambda t: (t, 0, 0)), whole, whole]
    if before is not None:
        args.append(before)
        in_specs.append(whole)
    return pl.pallas_call(
        functools.partial(attend_back_kernel, before is not None),
        grid=(tens,),
        in_specs=in_specs,
        out_specs=[part, whole],
        out_shape=[
            jax.ShapeDtypeStruct((tens, 256, rows), BF16),
            jax.ShapeDtypeStruct((length // rows, 2 * HD, rows), F32),
        ],
        scratch_shapes=[
            pltpu.VMEM((length, HD), BF16),
            pltpu.VMEM((length, HD), BF16),
            pltpu.VMEM((HD, length), BF16),
            pltpu.VMEM((length, HD), F32),
            pltpu.VMEM((length, HD), F32),
        ],
        compiler_params=pltpu.CompilerParams(vmem_limit_bytes=56 * MIB),
    )(*args)


def norm_back_kernel(first, gx_ref, x_ref, norm_ref, mlp_ref, gqt_ref, qk_ref, *rest):
    if first:
        ov_ref, dkv_ref, trig_ref, out_ref, pack_ref, sums_ref, normed_t, attn, shared = rest
    else:
        out_ref, pack_ref, sums_ref, normed_t, attn = rest
    t = pl.program_id(0)

    @pl.when(t == 0)
    def _():
        x = x_ref[...].astype(F32)
        normed = (standard(x)[0] * norm_ref[0:1] + norm_ref[1:2]).astype(BF16)
        normed_t[...] = turn(normed).astype(BF16)
        if first:
            cos, sin = trig_ref[0:HALF], trig_ref[HALF:ROT]
            grad = dkv_ref[...]
            shared[:ROT] = rotated(grad[:ROT], cos, -sin).astype(BF16)
            shared[ROT:] = grad[ROT:].astype(BF16)
            attn[...] = dot_nt(turn(shared[:HD]).astype(BF16), qk_ref[0, :, QW:]) + dot_nt(
                turn(shared[HD:]).astype(BF16), ov_ref[0, :, QW:]
            )
        else:
            attn[...] = jnp.zeros_like(attn)

    grad_t = gqt_ref[0, :QW]
    attn[...] += dot_nt(turn(grad_t).astype(BF16), qk_ref[0, :, :QW])
    if first:
        left = jnp.concatenate([grad_t, shared[:HD]], axis=0)
        pack_ref[0, :, :256] = dot_nt(normed_t[...], left).astype(BF16)
        right = jnp.concatenate([shared[HD:], jnp.zeros((HD, grad_t.shape[1]), BF16)], axis=0)
        pack_ref[0, :, 256:] = dot_nt(normed_t[...], right).astype(BF16)
    else:
        pack_ref[0] = dot_nt(normed_t[...], gqt_ref[0]).astype(BF16)

    @pl.when(t == pl.num_programs(0) - 1)
    def _():
        unit, inverse = standard(x_ref[...].astype(F32))
        attn_grad, mlp_grad = attn[...], mlp_ref[...]
        sums_ref[0:1] = jnp.sum(attn_grad * unit, axis=0, keepdims=True)
        sums_ref[1:2] = jnp.sum(attn_grad, axis=0, keepdims=True)
        sums_ref[2:3] = jnp.sum(mlp_grad * unit, axis=0, keepdims=True)
        sums_ref[3:4] = jnp.sum(mlp_grad, axis=0, keepdims=True)
        grad = attn_grad * norm_ref[0:1] + mlp_grad * norm_ref[2:3]
        mean = jnp.mean(grad, axis=-1, keepdims=True)
        slant = jnp.mean(grad * unit, axis=-1, keepdims=True)
        out_ref[...] = gx_ref[...] + inverse * (grad - mean - unit * slant)


def norm_back_call(first, gx, x, norms, mlp, gqt, weights, dkv=None, trig=None):
    rows, width = x.shape
    tens = weights.shape[0]
    whole = pl.BlockSpec(memory_space=pltpu.VMEM)
    part = pl.BlockSpec((1, 256, rows), lambda t: (t, 0, 0))
    args = [gx, x, norms, mlp, gqt, weights]
    in_specs = [whole] * 4 + [part, pl.BlockSpec((1, width, 256), lambda t: (t, 0, 6))]
    scratch = [pltpu.VMEM((width, rows), BF16), pltpu.VMEM((rows, width), F32)]
    cols = 256
    if first:
        args += [weights, dkv, trig]
        in_specs += [pl.BlockSpec((1, width, 256), lambda t: (0, 0, 7)), whole, whole]
        scratch.append(pltpu.VMEM((2 * HD, rows), BF16))
        cols = 384
    return pl.pallas_call(
        functools.partial(norm_back_kernel, first),
        grid=(tens,),
        in_specs=in_specs,
        out_specs=[whole, pl.BlockSpec((1, width, cols), lambda t: (t, 0, 0)), whole],
        out_shape=[
            jax.ShapeDtypeStruct((rows, width), F32),
            jax.ShapeDtypeStruct((tens, width, cols), BF16),
            jax.ShapeDtypeStruct((4, width), F32),
        ],
        scratch_shapes=scratch,
        compiler_params=pltpu.CompilerParams(vmem_limit_bytes=48 * MIB),
    )(*args)


def tensor_barrier(count):
    me = lax.axis_index("tensor")
    barrier = pltpu.get_barrier_semaphore()
    for shift in range(1, count):
        pl.semaphore_signal(
            barrier, inc=1, device_id={"tensor": lax.rem(me + shift, count)}, device_id_type=MESH
        )
    pl.semaphore_wait(barrier, count - 1)


def share_kernel(count, mine_ref, out_ref, here_sem, send_sem, recv_sem):
    me = lax.axis_index("tensor")
    tensor_barrier(count)
    copies = []
    for shift in range(1, count):
        copies.append(
            pltpu.make_async_remote_copy(
                src_ref=mine_ref,
                dst_ref=out_ref.at[me],
                send_sem=send_sem.at[shift],
                recv_sem=recv_sem.at[shift],
                device_id={"tensor": lax.rem(me + shift, count)},
                device_id_type=MESH,
            )
        )
        copies[-1].start()
    own = pltpu.make_async_copy(mine_ref, out_ref.at[me], here_sem)
    own.start()
    own.wait()
    for copy in copies:
        copy.wait()


def share_call(mine, count):
    return pl.pallas_call(
        functools.partial(share_kernel, count),
        in_specs=[pl.BlockSpec(memory_space=pltpu.VMEM)],
        out_specs=pl.BlockSpec(memory_space=pltpu.VMEM),
        out_shape=jax.ShapeDtypeStruct((count,) + mine.shape, mine.dtype),
        scratch_shapes=[
            pltpu.SemaphoreType.DMA,
            pltpu.SemaphoreType.DMA((count,)),
            pltpu.SemaphoreType.DMA((count,)),
        ],
        compiler_params=pltpu.CompilerParams(collective_id=1, has_side_effects=True),
    )(mine)


def merge_kernel(count, parts_ref, out_ref, low, landed, send_sem, recv_sem):
    me = lax.axis_index("tensor")
    low[...] = parts_ref[...].astype(BF16)
    tensor_barrier(count)
    copies = []
    for shift in range(1, count):
        to = lax.rem(me + shift, count)
        copies.append(
            pltpu.make_async_remote_copy(
                src_ref=low.at[to],
                dst_ref=landed.at[shift],
                send_sem=send_sem.at[shift],
                recv_sem=recv_sem.at[shift],
                device_id={"tensor": to},
                device_id_type=MESH,
            )
        )
        copies[-1].start()
    total = parts_ref[me]
    for shift, copy in enumerate(copies, 1):
        copy.wait()
        total = total + landed[shift].astype(F32)
    out_ref[...] = total


def merge_call(parts):
    count = parts.shape[0]
    vmem = pl.BlockSpec(memory_space=pltpu.VMEM)
    return pl.pallas_call(
        functools.partial(merge_kernel, count),
        in_specs=[vmem],
        out_specs=vmem,
        out_shape=jax.ShapeDtypeStruct(parts.shape[1:], F32),
        scratch_shapes=[
            pltpu.VMEM(parts.shape, BF16),
            pltpu.VMEM(parts.shape, BF16),
            pltpu.SemaphoreType.DMA((count,)),
            pltpu.SemaphoreType.DMA((count,)),
        ],
        compiler_params=pltpu.CompilerParams(collective_id=2, has_side_effects=True),
    )(parts)


class Place:
    def __init__(self):
        dp, tensor = lax.axis_index("dp"), lax.axis_index("tensor")
        self.z, self.x = dp // 2, lax.rem(dp, 2)
        self.y, self.core = tensor // 2, lax.rem(tensor, 2)

    def at(self, z=None, x=None, y=None, core=None):
        z = self.z if z is None else z
        x = self.x if x is None else x
        y = self.y if y is None else y
        core = self.core if core is None else core
        return (z * 2 + x, y * 2 + core)

    def peers(self):
        near = [self.at(x=1 - self.x), self.at(y=1 - self.y), self.at(core=1 - self.core)]
        return near + [self.at(z=lax.rem(self.z + d, 4)) for d in (1, 2, 3)]

    def greet(self):
        barrier = pltpu.get_barrier_semaphore()
        for peer in self.peers():
            pl.semaphore_signal(barrier, inc=1, device_id=peer, device_id_type=MESH)
        pl.semaphore_wait(barrier, 6)


def push(src, dst, send, recv, to):
    copy = pltpu.make_async_remote_copy(
        src_ref=src, dst_ref=dst, send_sem=send, recv_sem=recv, device_id=to, device_id_type=MESH
    )
    copy.start()
    return copy


def gather_kernel(packs, *refs):
    sources, small = refs[:packs], refs[packs]
    outs, small_out = refs[packs + 1 : 2 * packs + 1], refs[2 * packs + 1]
    own_sem, send, recv, small_send, small_recv = refs[2 * packs + 2 :]
    me = Place()
    tensor = me.y * 2 + me.core
    other = (1 - me.y) * 2 + me.core
    ahead = [lax.rem(me.z + 4 - d, 4) for d in range(4)]
    to_x, to_y, to_core = me.at(x=1 - me.x), me.at(y=1 - me.y), me.at(core=1 - me.core)
    half = sources[0].shape[0] // 2
    me.greet()

    small_copies = [
        push(
            small, small_out.at[me.x, me.z], small_send.at[d], small_recv.at[d],
            me.at(z=lax.rem(me.z + d, 4)),
        )
        for d in (1, 2, 3)
    ]
    own = [pltpu.make_async_copy(small, small_out.at[me.x, me.z], own_sem.at[packs])]
    own[0].start()
    along = []
    for k in range(packs):
        copy = pltpu.make_async_copy(sources[k], outs[k].at[tensor, me.z, me.x], own_sem.at[k])
        copy.start()
        own.append(copy)
        along.append(
            [
                push(
                    sources[k], outs[k].at[tensor, me.z, me.x], send.at[k, d - 1],
                    recv.at[k, d - 1], me.at(z=lax.rem(me.z + d, 4)),
                )
                for d in (1, 2, 3)
            ]
        )
    for copy in own:
        copy.wait()
    done = []
    for copy in small_copies:
        copy.wait_recv()
    done += small_copies
    last = push(
        small_out.at[me.x], small_out.at[me.x], small_send.at[0], small_recv.at[0], to_x
    )
    for k in range(packs):
        out = outs[k]
        x_copies, y_copies, core_copies = [], [], []
        for d in range(4):
            z = ahead[d]
            if d > 0:
                along[k][d - 1].wait_recv()
            block = out.at[tensor, z, me.x]
            x_copies.append(push(block, block, send.at[k, 3 + d], recv.at[k, 3 + d], to_x))
            y_copies.append(push(block, block, send.at[k, 7 + d], recv.at[k, 7 + d], to_y))
            core_copies.append(push(block, block, send.at[k, 11 + d], recv.at[k, 11 + d], to_core))
        cross = []
        for d in range(4):
            z = ahead[d]
            x_copies[d].wait_recv()
            from_x = out.at[tensor, z, 1 - me.x]
            top = out.at[tensor, z, 1 - me.x, pl.ds(0, half)]
            cross.append(push(top, top, send.at[k, 15 + d], recv.at[k, 15 + d], to_y))
            core_copies.append(
                push(from_x, from_x, send.at[k, 19 + d], recv.at[k, 19 + d], to_core)
            )
            y_copies[d].wait_recv()
            from_y = out.at[other, z, me.x]
            low = out.at[other, z, me.x, pl.ds(half, half)]
            cross.append(push(low, low, send.at[k, 23 + d], recv.at[k, 23 + d], to_x))
            core_copies.append(
                push(from_y, from_y, send.at[k, 27 + d], recv.at[k, 27 + d], to_core)
            )
        for d in range(4):
            z = ahead[d]
            cross[2 * d].wait_recv()
            cross[2 * d + 1].wait_recv()
            block = out.at[other, z, 1 - me.x]
            core_copies.append(push(block, block, send.at[k, 31 + d], recv.at[k, 31 + d], to_core))
        for copy in core_copies:
            copy.wait_recv()
        done += along[k] + x_copies + y_copies + cross + core_copies
    last.wait_recv()
    done.append(last)
    for copy in done:
        copy.wait_send()


def gather_call(packs, small):
    count = len(packs)
    anywhere = pl.BlockSpec(memory_space=pl.ANY)
    outs = pl.pallas_call(
        functools.partial(gather_kernel, count),
        in_specs=[anywhere] * (count + 1),
        out_specs=[anywhere] * (count + 1),
        out_shape=[jax.ShapeDtypeStruct((4, 4, 2) + pack.shape, pack.dtype) for pack in packs]
        + [jax.ShapeDtypeStruct((2, 4) + small.shape, small.dtype)],
        scratch_shapes=[
            pltpu.SemaphoreType.DMA((count + 1,)),
            pltpu.SemaphoreType.DMA((count, 35)),
            pltpu.SemaphoreType.DMA((count, 35)),
            pltpu.SemaphoreType.DMA((4,)),
            pltpu.SemaphoreType.DMA((4,)),
        ],
        compiler_params=pltpu.CompilerParams(collective_id=3, has_side_effects=True),
    )(*packs, small)
    return outs[:count], jnp.swapaxes(outs[count], 0, 1)


def scatter_kernel(parts_ref, out_ref, total, from_core, from_x, from_y, turn_x, turn_y, from_z, send, recv):
    me = Place()
    half = parts_ref.shape[3] // 2
    to_x, to_y, to_core = me.at(x=1 - me.x), me.at(y=1 - me.y), me.at(core=1 - me.core)
    top, low = pl.ds(0, half), pl.ds(half, half)
    order = [lax.rem(me.z + d, 4) for d in (1, 2, 3, 0)]
    me.greet()
    core_copies, x_copies, y_copies, x_turns, y_turns, z_copies = [], [], [], [], [], []
    for d, z in enumerate(order):
        for y in range(2):
            core_copies.append(
                push(
                    parts_ref.at[2 * y + 1 - me.core, z], from_core.at[y, z],
                    send.at[2 * d + y], recv.at[2 * d + y], to_core,
                )
            )
    for d, z in enumerate(order):
        for y in range(2):
            core_copies[2 * d + y].wait_recv()
            for x in range(2):
                total[z, x, y] = parts_ref[2 * y + me.core, z, x] + from_core[y, z, x]
        x_copies.append(
            push(
                total.at[z, 1 - me.x, :, top], from_x.at[z], send.at[8 + d], recv.at[8 + d], to_x
            )
        )
        y_copies.append(
            push(
                total.at[z, :, 1 - me.y, low], from_y.at[z], send.at[12 + d], recv.at[12 + d], to_y
            )
        )
    for d, z in enumerate(order):
        x_copies[d].wait_recv()
        for y in range(2):
            total[z, me.x, y, top] += from_x[z, y]
        y_turns.append(
            push(
                total.at[z, me.x, 1 - me.y, top], turn_y.at[z],
                send.at[16 + d], recv.at[16 + d], to_y,
            )
        )
        y_copies[d].wait_recv()
        for x in range(2):
            total[z, x, me.y, low] += from_y[z, x]
        x_turns.append(
            push(
                total.at[z, 1 - me.x, me.y, low], turn_x.at[z],
                send.at[20 + d], recv.at[20 + d], to_x,
            )
        )
    for d, z in enumerate(order):
        y_turns[d].wait_recv()
        total[z, me.x, me.y, top] += turn_y[z]
        x_turns[d].wait_recv()
        total[z, me.x, me.y, low] += turn_x[z]
        if d < 3:
            z_copies.append(
                push(
                    total.at[z, me.x, me.y], from_z.at[d],
                    send.at[24 + d], recv.at[24 + d], me.at(z=z),
                )
            )
    result = total[me.z, me.x, me.y].astype(F32)
    for d, copy in enumerate(z_copies):
        copy.wait_recv()
        result = result + from_z[d].astype(F32)
    out_ref[...] = result
    for copy in core_copies + x_copies + y_copies + x_turns + y_turns + z_copies:
        copy.wait_send()


def scatter_call(parts, ident):
    tens, width, cols = parts.shape
    rows = width // 8
    half = rows // 2
    parts = parts.reshape(tens, 4, 2, rows, cols)
    vmem = pl.BlockSpec(memory_space=pltpu.VMEM)
    return pl.pallas_call(
        scatter_kernel,
        in_specs=[vmem],
        out_specs=vmem,
        out_shape=jax.ShapeDtypeStruct((rows, cols), F32),
        scratch_shapes=[
            pltpu.VMEM((4, 2, 2, rows, cols), BF16),
            pltpu.VMEM((2, 4, 2, rows, cols), BF16),
            pltpu.VMEM((4, 2, half, cols), BF16),
            pltpu.VMEM((4, 2, half, cols), BF16),
            pltpu.VMEM((4, half, cols), BF16),
            pltpu.VMEM((4, half, cols), BF16),
            pltpu.VMEM((3, rows, cols), BF16),
            pltpu.SemaphoreType.DMA((27,)),
            pltpu.SemaphoreType.DMA((27,)),
        ],
        compiler_params=pltpu.CompilerParams(
            collective_id=ident, has_side_effects=True, vmem_limit_bytes=56 * MIB
        ),
    )(parts)


def angles(places):
    steps = jnp.arange(HALF).astype(F32)
    inverse = jnp.exp(steps * (-2.0 * math.log(10000.0) / ROT))
    phase = (0.25 * inverse)[:, None] * places.astype(F32)[None, :]
    return jnp.concatenate([jnp.cos(phase), jnp.sin(phase)], axis=0)


def param_squares(arrays, leader):
    query, keyval, output, upward, downward, norms = arrays
    return jnp.concatenate(
        [
            jnp.sum(query * query, axis=(1, 2)),
            (jnp.sum(keyval * keyval) * leader)[None],
            jnp.sum(output * output, axis=(1, 2)),
            jnp.sum(upward * upward, axis=(1, 2)),
            jnp.sum(downward * downward, axis=(1, 2)),
            jnp.sum(norms * norms, axis=2).reshape(8) * leader,
        ]
    )


def lamb_parts(weight, first, second, grad):
    first_new = BETA_FIRST * first + (1.0 - BETA_FIRST) * grad
    second_new = BETA_SECOND * second + (1.0 - BETA_SECOND) * grad * grad
    update = (
        first_new
        / (1.0 - BETA_FIRST**STEP)
        / (jnp.sqrt(second_new / (1.0 - BETA_SECOND**STEP)) + ADAM_EPSILON)
        + WEIGHT_DECAY * weight
    )
    return (first_new, second_new, update)


def apply_trust(masters, updates, trust):
    factors = (
        trust[0:2][:, None, None],
        trust[2],
        trust[3:5][:, None, None],
        trust[5:7][:, None, None],
        trust[7:9][:, None, None],
        trust[9:17].reshape(2, 4, 1),
    )
    return tuple(
        (
            weight - LEARN_RATE * factor * update
            for weight, factor, update in zip(masters, factors, updates)
        )
    )


def shards(
    fast,
    hidden_in,
    out_grad,
    positions,
    query_weight,
    keyval_weight,
    output_weight,
    up_weight,
    down_weight,
    norm_params,
    query_first,
    query_second,
    keyval_first,
    keyval_second,
    output_first,
    output_second,
    up_first,
    up_second,
    down_first,
    down_second,
    norm_first,
    norm_second,
):
    masters = (query_weight, keyval_weight, output_weight, up_weight, down_weight, norm_params)
    tensor = lax.axis_index("tensor")
    leader = (tensor == 0).astype(F32)
    rows, width = hidden_in.shape
    tens = positions.shape[0] // rows
    depth = keyval_weight.shape[0]

    packs = []
    for layer in range(2):
        if layer == 0:
            keys, values = keyval_weight[:, :HD], keyval_weight[:, HD:]
        else:
            keys = values = jnp.zeros((depth, HD), F32)
        packs.append(
            jnp.concatenate(
                [
                    up_weight[layer],
                    down_weight[layer].T,
                    query_weight[layer],
                    keys,
                    output_weight[layer].T,
                    values,
                ],
                axis=1,
            ).astype(BF16)
        )
    norm_low = norm_params.astype(BF16).reshape(8, depth)
    if fast:
        norm_pack = jnp.pad(norm_low, ((0, 8), (0, 128 - depth)))
        weights, norm_all = gather_call(packs, norm_pack)
        weights = [w.reshape(tens, width, w.shape[-1]) for w in weights]
        norm_full = norm_all[:, :, :8, :depth].reshape(-1, 8, depth)
    else:
        weights = [
            lax.all_gather(pack, ("tensor", "dp"), axis=0).reshape(tens, width, pack.shape[1])
            for pack in packs
        ]
        norm_full = lax.all_gather(norm_low, "dp", axis=0)
    norm_full = jnp.swapaxes(norm_full, 0, 1).reshape(2, 4, width).astype(F32)
    trig = angles(lax.dynamic_slice_in_dim(positions, tensor * rows, rows, 0))

    current = hidden_in
    saved = []
    kv = None
    for layer in range(2):
        norms = norm_full[layer]
        if layer == 0:
            qt, kv_here = qkv_call(True, current, norms, trig, weights[layer])
            kv = share_call(kv_here, tens).reshape(-1, 2 * HD)
        else:
            (qt,) = qkv_call(False, current, norms, trig, weights[layer])
        at, lse = attend_call(qt, kv)
        after, act, slope = mix_call(current, norms, at, weights[layer])
        saved.append((current, qt, at, lse, act, slope))
        current = after

    grad = out_grad
    dkv = None
    early, late, sums = [None, None], [None, None], [None, None]
    for layer in (1, 0):
        norms = norm_full[layer]
        x, qt, at, lse, act, slope = saved[layer]
        early[layer], dout, mlp = mix_back_call(grad, x, norms, at, act, slope, weights[layer])
        gqt, dkv = attend_back_call(qt, dout, at, lse, kv, trig, dkv)
        if layer == 0:
            dkv = merge_call(dkv)
        grad, late[layer], sums[layer] = norm_back_call(
            layer == 0, grad, x, norms, mlp, gqt, weights[layer],
            dkv if layer == 0 else None, trig if layer == 0 else None,
        )
    sums_t = jnp.concatenate(sums, axis=0).T.astype(BF16)
    late[0] = lax.dynamic_update_slice(
        late[0], jnp.broadcast_to(sums_t[None], (tens,) + sums_t.shape), (0, 0, 256 + HD)
    )

    def scatter(parts, ident):
        if fast:
            return scatter_call(parts, ident)
        pieces = parts.reshape(-1, depth, parts.shape[-1])
        return lax.psum_scatter(
            pieces, ("tensor", "dp"), scatter_dimension=0, tiled=False
        ).astype(F32)

    early = [scatter(early[layer], 4) for layer in range(2)]
    late = [scatter(late[layer], 5 + layer) for layer in range(2)]
    hidden = up_weight.shape[2]
    query_g = jnp.stack([late[layer][:, :QW] for layer in range(2)])
    keyval_g = late[0][:, QW : QW + 2 * HD]
    output_g = jnp.stack([early[layer][:, 2 * hidden : 2 * hidden + QW].T for layer in range(2)])
    up_g = jnp.stack([early[layer][:, :hidden] for layer in range(2)])
    down_g = jnp.stack([early[layer][:, hidden : 2 * hidden].T for layer in range(2)])
    norm_g = late[0][:, QW + 2 * HD : QW + 2 * HD + 8].T.reshape(2, 4, depth)

    grads = (query_g, keyval_g, output_g, up_g, down_g, norm_g)
    firsts = (query_first, keyval_first, output_first, up_first, down_first, norm_first)
    seconds = (query_second, keyval_second, output_second, up_second, down_second, norm_second)
    parts = [
        lamb_parts(weight, first, second, grad)
        for weight, first, second, grad in zip(masters, firsts, seconds, grads)
    ]
    updates = tuple((part[2] for part in parts))
    weight_total, update_total = lax.psum(
        (param_squares(masters, leader), param_squares(updates, leader)), ("dp", "tensor")
    )
    weight_norm = jnp.sqrt(weight_total)
    update_norms = jnp.sqrt(update_total)
    trust_ratios = weight_norm / update_norms
    nexts = apply_trust(masters, updates, trust_ratios)
    outs = [current, grad]
    for index in range(6):
        low = nexts[index].astype(BF16)
        outs += [parts[index][0], parts[index][1], nexts[index], low]
    return tuple(outs) + (update_norms, trust_ratios)


def solution(mesh):
    fast = mesh.shape["dp"] == 8 and mesh.shape["tensor"] == 4
    columns = P(None, "dp", "tensor")
    across = P(None, "tensor", "dp")
    flat = P("dp", None)
    norm = P(None, None, "dp")
    state = P(("dp", "tensor"), None)
    in_specs = (
        (state, state, P("dp"), columns, flat, across, columns, across, norm)
        + (columns, columns, flat, flat, across, across, columns, columns, across, across)
        + (norm, norm)
    )
    out_specs = (
        (state, state)
        + (columns,) * 4
        + (flat,) * 4
        + (across,) * 4
        + (columns,) * 4
        + (across,) * 4
        + (norm,) * 4
        + (P(), P())
    )
    return jax.shard_map(
        functools.partial(shards, fast),
        mesh=mesh,
        in_specs=in_specs,
        out_specs=out_specs,
        check_vma=False,
    )
```

time: 1760 us -> 697 us (0.40)
  waiting for transfers between devices: 743 us -> 0 us
  Pallas kernels: 0 us -> 570 us
  matrix products: 417 us -> 0 us
  other arithmetic: 172 us -> 22.5 us
  blocking collectives: 183 us -> 45.5 us
  local copies, waits for them, and re-layouts: 175 us -> 44.6 us
  loops' own time: 38.6 us -> 0 us
    pallas_call x0 -> x19, Pallas kernels: none -> 570 us  [the longest x4 191 us: scatter_call(): pl.pallas_call(scatter_kernel, in_specs=[vmem], out_specs=vmem, out_shape...]
    dot_general x91 -> x0, matrix products: 417 us -> none  [the longest x16 77.6 us: masked_scores(): jnp.einsum('qhd,kd->hqk', query_block, keys, preferred_element_type=jnp.f...]
    unnamed x25 -> x0, waiting for transfers between devices: 338 us -> none
    reduce_scatter x9 -> x0, waiting for transfers between devices: 325 us -> none  [the longest x2 112 us: shards(): lax.psum_scatter(term, 'tensor', scatter_dimension=0, tiled=True)]
    all_gather x4 -> x0, blocking collectives: 131 us -> none  [the longest x1 34.4 us: shards(): lax.all_gather(query_weight.astype(jnp.bfloat16), 'dp', axis=1, tiled=True)]
    all_gather x8 -> x0, waiting for transfers between devices: 80.7 us -> none  [the longest x2 53.5 us: shards(): lax.all_gather(grad_state.astype(jnp.bfloat16), 'tensor', axis=0, tiled=T...]
    reduce_sum x15 -> x0, other arithmetic: 67.3 us -> none  [the longest x8 54.2 us: one(): total = jnp.sum(weights, axis=-1, keepdims=True)]
    dynamic_update_slice x16 -> x1, local copies, waits for them, and re-layouts: 72.1 us -> 10.8 us  [shards(): lax.dynamic_update_slice(late[0], jnp.broadcast_to(sums_t[None], (tens,)...]
  transfers between devices with their start and end apart: 21 -> 0, of which waited for: 14 -> 0; matrix products, arithmetic and copies ran while one was open for 30% -> 0% of each run, Pallas kernels for 0% -> 0%
where the time goes in v1:
time: 697 us; the launch traced here: 686 us
  Pallas kernels  570 us (82%)
  blocking collectives  45.5 us (7%)
  local copies, waits for them, and re-layouts  44.6 us (6%)
  other arithmetic  22.5 us (3%)
    pallas_call x4, Pallas kernels, scatter_call(): pl.pallas_call(scatter_kernel, in_specs=[vmem], out_specs=vmem, out_shape...  191 us
    pallas_call x1, Pallas kernels, gather_call(): pl.pallas_call(functools.partial(gather_kernel, count), in_specs=[anywher...  140 us
    pallas_call x1, Pallas kernels, merge_call(): pl.pallas_call(functools.partial(merge_kernel, count), in_specs=[vmem], o...  102 us
    psum x1, blocking collectives, shards(): lax.psum((param_squares(masters, leader), param_squares(updates, leader))...  45.5 us
    pallas_call x2, Pallas kernels, mix_back_call(): pl.pallas_call(mix_back_kernel, grid=(tens,), in_specs=[whole, whole, who...  37.1 us
    pallas_call x2, Pallas kernels, mix_call(): pl.pallas_call(mix_kernel, grid=(tens,), in_specs=[whole, whole, pl.Block...  31.5 us
    pallas_call x2, Pallas kernels, attend_back_call(): pl.pallas_call(functools.partial(attend_back_kernel, before is not None),...  25.2 us
    unnamed x113, local copies, waits for them, and re-layouts  24.5 us

profile of v1, /device:TPU:0, one launch (start us, length us, event | category | flops | bytes accessed | tf_op | source)
XLA Modules:
  0.0 686.3 jit_solution(17051609973164517040)
XLA Ops:
  6.3 140.2 %shard_map.420 = (bf16[4,4,2,96,2048]{4,3,2,1,0:T(8,128)(2,1)}, bf16[4,4,2,96,2048]{4,3,2,1,0:T(8,128)(2,1)}, bf16[2,4,16,128]{3,2,1,0:T(8,128)(2,1)}) custom-call(bf16[96,2048]{1,0:T(8,128)(2,1)} %concatenate.21.refs_0_, bf16[96,2048]{1,0:T(8,128)(2,1)} %concatenate.22.refs_1_, bf16[16,128]{1,0:T(8,128)(2,1)} %pad.4.refs_2_), custom_call_target="tpu_custom_call" | custom-call | tf_op jit(solution)/shard_map/pallas_call | solution.py:704
  148.3 4.6 copy-done
  152.8 3.2 shard_map.421
  156.7 8.6 %shard_map.422 = bf16[4,512,128]{2,1,0:T(8,128)(2,1)} custom-call(bf16[512,128]{1,0:T(8,128)(2,1)} %copy-done.26), custom_call_target="tpu_custom_call" | custom-call | tf_op jit(solution)/shard_map/pallas_call | solution.py:525
  166.3 6.0 shard_map.423
  172.9 15.6 %shard_map.424 = (f32[512,768]{1,0:T(8,128)S(1)}, bf16[4,512,768]{2,1,0:T(8,128)(2,1)}, bf16[4,512,768]{2,1,0:T(8,128)(2,1)}) custom-call(bf16[512,768]{1,0:T(8,128)(2,1)S(1)} %copy-done.5, f32[4,768]{1,0:T(4,128)S(1)} %squeeze.49.norm_ref, bf16[4,256,512]{2,1,0:T(8,128)(2,1)S(1)} %get-tuple-element.63.at_ref, bf16[4,768,2048]{2,1,0:T(8,128)(2,1)} %bitcast.68, ...), custom_call_target="tpu_custom_call" | custom-call | tf_op jit(solution)/shard_map/pallas_call | solution.py:218
  188.7 5.1 copy-done.1
  193.7 2.6 shard_map.425.qt_ref
  196.3 6.0 shard_map.426
  202.3 15.9 %shard_map.427 = (f32[512,768]{1,0:T(8,128)}, bf16[4,512,768]{2,1,0:T(8,128)(2,1)S(1)}, bf16[4,512,768]{2,1,0:T(8,128)(2,1)}) custom-call(f32[512,768]{1,0:T(8,128)S(1)} %get-tuple-element.64.x_ref, f32[4,768]{1,0:T(4,128)S(1)} %squeeze.50.norm_ref, bf16[4,256,512]{2,1,0:T(8,128)(2,1)S(1)} %get-tuple-element.66.at_ref, bf16[4,768,2048]{2,1,0:T(8,128)(2,1)} %bitcast.78, ...), custom_call_target="tpu_custom_call" | custom-call | tf_op jit(solution)/shard_map/pallas_call | solution.py:218
  218.2 1.6 copy-done.14
  219.8 18.7 %shard_map.428 = (bf16[4,768,1792]{2,1,0:T(8,128)(2,1)}, bf16[4,256,512]{2,1,0:T(8,128)(2,1)}, f32[512,768]{1,0:T(8,128)}) custom-call(f32[512,768]{1,0:T(8,128)} %gx_ref.3, f32[512,768]{1,0:T(8,128)} %copy-done.2, f32[4,768]{1,0:T(4,128)} %copy-done.24, bf16[4,256,512]{2,1,0:T(8,128)(2,1)} %copy-done.9, bf16[4,512,768]{2,1,0:T(8,128)(2,1)} %copy-done.14, ...), custom_call_target="tpu_custom_call" | custom-call | tf_op jit(solution)/shard_map/pallas_call | solution.py:274
  238.5 12.4 %shard_map.429 = (bf16[4,256,512]{2,1,0:T(8,128)(2,1)}, f32[4,128,512]{2,1,0:T(8,128)}) custom-call(bf16[4,256,512]{2,1,0:T(8,128)(2,1)} %copy-done.8, bf16[4,256,512]{2,1,0:T(8,128)(2,1)} %get-tuple-element.71.dot_ref, bf16[4,256,512]{2,1,0:T(8,128)(2,1)} %copy-done.9, f32[4,8,512]{2,1,0:T(8,128)} %copy-done.28, bf16[2048,128]{1,0:T(8,128)(2,1)} %bitcast.86, ...), custom_call_target="tpu_custom_call" | custom-call | tf_op jit(solution)/shard_map/pallas_call | solution.py:395
  252.2 7.2 %shard_map.430 = (f32[512,768]{1,0:T(8,128)S(1)}, bf16[4,768,256]{2,1,0:T(8,128)(2,1)S(1)}, f32[4,768]{1,0:T(4,128)S(1)}) custom-call(f32[512,768]{1,0:T(8,128)S(1)} %copy-done.12, f32[512,768]{1,0:T(8,128)} %copy-done.2, f32[4,768]{1,0:T(4,128)S(1)} %copy-done.25, f32[512,768]{1,0:T(8,128)} %get-tuple-element.70.mlp_ref, ...), custom_call_target="tpu_custom_call" | custom-call | tf_op jit(solution)/shard_map/pallas_call | solution.py:476
  260.6 1.2 copy-done.15
  261.8 18.5 %shard_map.431 = (bf16[4,768,1792]{2,1,0:T(8,128)(2,1)}, bf16[4,256,512]{2,1,0:T(8,128)(2,1)}, f32[512,768]{1,0:T(8,128)}) custom-call(f32[512,768]{1,0:T(8,128)} %copy-done.10, bf16[512,768]{1,0:T(8,128)(2,1)} %x_ref.7, f32[4,768]{1,0:T(4,128)} %copy-done.22, bf16[4,256,512]{2,1,0:T(8,128)(2,1)} %copy-done.7, ...), custom_call_target="tpu_custom_call" | custom-call | tf_op jit(solution)/shard_map/pallas_call | solution.py:274
  280.3 12.8 %shard_map.432 = (bf16[4,256,512]{2,1,0:T(8,128)(2,1)}, f32[4,128,512]{2,1,0:T(8,128)}) custom-call(bf16[4,256,512]{2,1,0:T(8,128)(2,1)} %copy-done.13, bf16[4,256,512]{2,1,0:T(8,128)(2,1)} %get-tuple-element.78.dot_ref, bf16[4,256,512]{2,1,0:T(8,128)(2,1)} %copy-done.7, f32[4,8,512]{2,1,0:T(8,128)} %copy-done.27, bf16[2048,128]{1,0:T(8,128)(2,1)} %bitcast.87, ...), custom_call_target="tpu_custom_call" | custom-call | tf_op jit(solution)/shard_map/pallas_call | solution.py:395
  293.1 102.5 %shard_map.433.rest_1_ = f32[128,512]{1,0:T(8,128)} custom-call(f32[4,128,512]{2,1,0:T(8,128)} %get-tuple-element.82.parts_ref), custom_call_target="tpu_custom_call" | custom-call | tf_op jit(solution)/shard_map/pallas_call | solution.py:567
  395.7 1.4 copy-done.16
  399.3 9.0 %shard_map.434 = (f32[512,768]{1,0:T(8,128)}, bf16[4,768,384]{2,1,0:T(8,128)(2,1)}, f32[4,768]{1,0:T(4,128)S(1)}) custom-call(f32[512,768]{1,0:T(8,128)S(1)} %copy-done.11, bf16[512,768]{1,0:T(8,128)(2,1)S(1)} %copy-done.6, f32[4,768]{1,0:T(4,128)S(1)} %copy-done.23, f32[512,768]{1,0:T(8,128)S(1)} %copy-done.16, bf16[4,256,512]{2,1,0:T(8,128)(2,1)S(1)} %copy-done.21, ...), custom_call_target="tpu_custom_call" | custom-call | tf_op jit(solution)/shard_map/pallas_call | solution.py:476
  408.2 19.3 %shard_map.436 = f32[96,256]{1,0:T(8,128)} custom-call(bf16[4,4,2,96,256]{4,3,2,1,0:T(8,128)(2,1)} %bitcast.90), custom_call_target="tpu_custom_call" | custom-call | tf_op jit(solution)/shard_map/pallas_call | solution.py:799
  427.9 10.8 %dynamic_update_slice.3 = bf16[4,768,384]{2,1,0:T(8,128)(2,1)} dynamic-update-slice(bf16[4,768,384]{2,1,0:T(8,128)(2,1)} %get-tuple-element.84, bf16[4,768,8]{2,1,0:T(8,128)(2,1)S(1)} %broadcast_in_dim.9, s32[]{:T(128)} %constant.29.clone.1, s32[]{:T(128)} %constant.29.clone.1, s32[]{:T(128)} %constant.31.clone.1) | dynamic-update-slice | bytes 98308 | tf_op jit(solution)/shard_map/dynamic_update_slice | solution.py:966
  438.8 22.8 %shard_map.435 = f32[96,384]{1,0:T(8,128)} custom-call(bf16[4,4,2,96,384]{4,3,2,1,0:T(8,128)(2,1)} %bitcast.93), custom_call_target="tpu_custom_call" | custom-call | tf_op jit(solution)/shard_map/pallas_call | solution.py:799
  463.5 2.2 multiply_reduce_fusion.8
  466.6 71.3 %shard_map.438 = f32[96,1792]{1,0:T(8,128)} custom-call(bf16[4,4,2,96,1792]{4,3,2,1,0:T(8,128)(2,1)} %bitcast.91), custom_call_target="tpu_custom_call" | custom-call | tf_op jit(solution)/shard_map/pallas_call | solution.py:799
  538.0 77.5 %shard_map.437 = f32[96,1792]{1,0:T(8,128)} custom-call(bf16[4,4,2,96,1792]{4,3,2,1,0:T(8,128)(2,1)} %bitcast.92), custom_call_target="tpu_custom_call" | custom-call | tf_op jit(solution)/shard_map/pallas_call | solution.py:799
  616.6 1.3 multiply_reduce_fusion.4
  619.2 2.0 multiply_reduce_fusion.1
  621.3 2.0 multiply_reduce_fusion
  628.3 45.5 %all-reduce.1 = (f32[17]{0:T(128)S(1)}, f32[17]{0:T(128)S(1)}) all-reduce(f32[17]{0:T(128)S(1)} %concatenate.26, f32[17]{0:T(128)S(1)} %concatenate.25), channel_id=1, replica_groups=mesh['dp'=8,'tensor'=4] {'dp','tensor'}, use_global_device_ids=true, to_apply=%region_13.14 | all-reduce | flops 34 | bytes 272 | tf_op jit(solution)/shard_map/psum | solution.py:996
  674.4 1.7 fusion.15
  677.4 1.4 fusion.14
  (161 shorter events, 31.5 us)
Async XLA Ops:
  1.9 3.8 copy-start.49
  3.0 145.2 %copy-start.5 = (bf16[512,768]{1,0:T(8,128)(2,1)S(1)}, bf16[512,768]{1,0:T(8,128)(2,1)}, u32[]{:S(2)}) copy-start(bf16[512,768]{1,0:T(8,128)(2,1)} %x_ref.7) | copy-start | bytes 2359300
  3.9 144.3 %copy-start.31 = (f32[2,192,96]{1,2,0:T(8,128)}, f32[2,192,96]{1,2,0:T(8,128)S(1)}, u32[]{:S(2)}) copy-start(f32[2,192,96]{1,2,0:T(8,128)S(1)} %copy.62) | copy-start | bytes 442372
  147.3 25.6 %copy-start.22 = (f32[4,768]{1,0:T(4,128)}, f32[4,768]{1,0:T(4,128)S(1)}, u32[]{:S(2)}) copy-start(f32[4,768]{1,0:T(4,128)S(1)} %squeeze.49.norm_ref) | copy-start | bytes 36868
  148.2 40.4 %copy-start.17 = (f32[16,512]{1,0:T(8,128)}, f32[16,512]{1,0:T(8,128)S(1)}, u32[]{:S(2)}) copy-start(f32[16,512]{1,0:T(8,128)S(1)} %pad_maximum_fusion.4.trig_ref.rest_2_) | copy-start | bytes 98308
  148.3 4.6 copy-start
  156.7 15.6 %copy-start.13 = (bf16[4,256,512]{2,1,0:T(8,128)(2,1)}, bf16[4,256,512]{2,1,0:T(8,128)(2,1)S(1)}, u32[]{:S(2)}) copy-start(bf16[4,256,512]{2,1,0:T(8,128)(2,1)S(1)} %get-tuple-element.61.qt_ref) | copy-start | bytes 3145732
  172.9 15.6 %copy-start.7 = (bf16[4,256,512]{2,1,0:T(8,128)(2,1)}, bf16[4,256,512]{2,1,0:T(8,128)(2,1)S(1)}, u32[]{:S(2)}) copy-start(bf16[4,256,512]{2,1,0:T(8,128)(2,1)S(1)} %get-tuple-element.63.at_ref) | copy-start | bytes 3145732
  188.6 13.8 %copy-start.2 = (f32[512,768]{1,0:T(8,128)}, f32[512,768]{1,0:T(8,128)S(1)}, u32[]{:S(2)}) copy-start(f32[512,768]{1,0:T(8,128)S(1)} %get-tuple-element.64.x_ref) | copy-start | bytes 4718596
  188.6 13.7 %copy-start.24 = (f32[4,768]{1,0:T(4,128)}, f32[4,768]{1,0:T(4,128)S(1)}, u32[]{:S(2)}) copy-start(f32[4,768]{1,0:T(4,128)S(1)} %squeeze.50.norm_ref) | copy-start | bytes 36868
  188.7 5.1 copy-start.1
  196.3 21.9 %copy-start.8 = (bf16[4,256,512]{2,1,0:T(8,128)(2,1)}, bf16[4,256,512]{2,1,0:T(8,128)(2,1)S(1)}, u32[]{:S(2)}) copy-start(bf16[4,256,512]{2,1,0:T(8,128)(2,1)S(1)} %shard_map.425.qt_ref) | copy-start | bytes 3145732
  202.3 15.9 %copy-start.9 = (bf16[4,256,512]{2,1,0:T(8,128)(2,1)}, bf16[4,256,512]{2,1,0:T(8,128)(2,1)S(1)}, u32[]{:S(2)}) copy-start(bf16[4,256,512]{2,1,0:T(8,128)(2,1)S(1)} %get-tuple-element.66.at_ref) | copy-start | bytes 3145732
  202.3 15.9 %copy-start.28 = (f32[4,8,512]{2,1,0:T(8,128)}, f32[4,8,512]{2,1,0:T(8,128)S(1)}, u32[]{:S(2)}) copy-start(f32[4,8,512]{2,1,0:T(8,128)S(1)} %get-tuple-element.72.lse_ref) | copy-start | bytes 196612
  238.5 12.5 %copy-start.12 = (f32[512,768]{1,0:T(8,128)S(1)}, f32[512,768]{1,0:T(8,128)}, u32[]{:S(2)}) copy-start(f32[512,768]{1,0:T(8,128)} %gx_ref.3) | copy-start | bytes 4718596
  238.5 12.5 %copy-start.25 = (f32[4,768]{1,0:T(4,128)S(1)}, f32[4,768]{1,0:T(4,128)}, u32[]{:S(2)}) copy-start(f32[4,768]{1,0:T(4,128)} %copy-done.24) | copy-start | bytes 36868
  280.3 115.3 %copy-start.6 = (bf16[512,768]{1,0:T(8,128)(2,1)S(1)}, bf16[512,768]{1,0:T(8,128)(2,1)}, u32[]{:S(2)}) copy-start(bf16[512,768]{1,0:T(8,128)(2,1)} %x_ref.7) | copy-start | bytes 2359300
  280.3 115.3 %copy-start.11 = (f32[512,768]{1,0:T(8,128)S(1)}, f32[512,768]{1,0:T(8,128)}, u32[]{:S(2)}) copy-start(f32[512,768]{1,0:T(8,128)} %copy-done.10) | copy-start | bytes 4718596
  280.3 115.3 %copy-start.18 = (f32[16,512]{1,0:T(8,128)S(1)}, f32[16,512]{1,0:T(8,128)}, u32[]{:S(2)}) copy-start(f32[16,512]{1,0:T(8,128)} %copy-done.17) | copy-start | bytes 98308
  280.3 115.3 %copy-start.23 = (f32[4,768]{1,0:T(4,128)S(1)}, f32[4,768]{1,0:T(4,128)}, u32[]{:S(2)}) copy-start(f32[4,768]{1,0:T(4,128)} %copy-done.22) | copy-start | bytes 36868
  427.8 33.8 %copy-start.42 = (f32[96,256]{1,0:T(8,128)S(1)}, f32[96,256]{1,0:T(8,128)}, u32[]{:S(2)}) copy-start(f32[96,256]{1,0:T(8,128)} %shard_map.436) | copy-start | bytes 294916
  427.9 34.6 %copy-start.43 = (f32[2,96,192]{2,1,0:T(8,128)S(1)}, f32[2,96,192]{2,1,0:T(8,128)}, u32[]{:S(2)}) copy-start(f32[2,96,192]{2,1,0:T(8,128)} %param.30) | copy-start | bytes 442372
  427.9 34.6 %copy-start.44 = (f32[2,96,192]{2,1,0:T(8,128)S(1)}, f32[2,96,192]{2,1,0:T(8,128)}, u32[]{:S(2)}) copy-start(f32[2,96,192]{2,1,0:T(8,128)} %param.31) | copy-start | bytes 442372
  438.7 24.7 %copy-start.47 = (f32[96,128]{1,0:T(8,128)S(1)}, f32[96,128]{1,0:T(8,128)}, u32[]{:S(2)}) copy-start(f32[96,128]{1,0:T(8,128)} %param.32) | copy-start | bytes 147460
  438.7 24.7 %copy-start.48 = (f32[96,128]{1,0:T(8,128)S(1)}, f32[96,128]{1,0:T(8,128)}, u32[]{:S(2)}) copy-start(f32[96,128]{1,0:T(8,128)} %param.33) | copy-start | bytes 147460
  438.7 27.6 %copy-start.45 = (f32[2,192,96]{2,1,0:T(8,128)S(1)}, f32[2,192,96]{2,1,0:T(8,128)}, u32[]{:S(2)}) copy-start(f32[2,192,96]{2,1,0:T(8,128)} %param.35) | copy-start | bytes 442372
  438.7 27.8 %copy-start.46 = (f32[2,192,96]{2,1,0:T(8,128)S(1)}, f32[2,192,96]{2,1,0:T(8,128)}, u32[]{:S(2)}) copy-start(f32[2,192,96]{2,1,0:T(8,128)} %param.34) | copy-start | bytes 442372
  537.9 77.6 %copy-start.33 = (f32[96,1792]{1,0:T(8,128)S(1)}, f32[96,1792]{1,0:T(8,128)}, u32[]{:S(2)}) copy-start(f32[96,1792]{1,0:T(8,128)} %shard_map.438) | copy-start | bytes 2064388
  538.0 78.6 %copy-start.32 = (f32[2,192,96]{1,2,0:T(8,128)S(1)}, f32[2,192,96]{1,2,0:T(8,128)}, u32[]{:S(2)}) copy-start(f32[2,192,96]{1,2,0:T(8,128)} %copy-done.31) | copy-start | bytes 442372
  615.5 3.6 copy-start.29
  621.2 56.1 %copy-start.41 = (f32[96,128]{1,0:T(8,128)S(1)}, f32[96,128]{1,0:T(8,128)}, u32[]{:S(2)}) copy-start(f32[96,128]{1,0:T(8,128)} %param.25) | copy-start | bytes 147460
  674.3 10.8 %copy-start.50 = (f32[17]{0:T(128)}, f32[17]{0:T(128)S(1)}, u32[]{:S(2)}) copy-start(f32[17]{0:T(128)S(1)} %get-tuple-element.160) | copy-start | bytes 208
  (21 other events, 41.8 us)

commit v2 on v0

v2 whole, which is shorter than its diff:
```python
import functools
import math

import jax
import jax.numpy as jnp
from jax import lax
from jax.experimental import pallas as pl
from jax.experimental.pallas import tpu as pltpu
from jax.sharding import PartitionSpec as P

F32 = jnp.float32
BF16 = jnp.bfloat16
MESH = pl.DeviceIdType.MESH

HD = 64
ROT = 16
HALF = ROT // 2
STEP = 5
HEADS_HERE = 3
QW = 192

NORM_EPSILON = 1e-05
BETA_FIRST = 0.5
BETA_SECOND = 0.55
ADAM_EPSILON = 1e-06
WEIGHT_DECAY = 0.01
LEARN_RATE = 0.5
SCALE = HD**-0.5
ROOM = 60 * 2**20


def dot(a, b):
    return jnp.dot(a, b, preferred_element_type=F32)


def dot_nt(a, b):
    return lax.dot_general(a, b, (((1,), (1,)), ((), ())), preferred_element_type=F32)


def turn(a):
    return jnp.transpose(a.astype(F32), (1, 0))


def standard(values):
    center = values - jnp.mean(values, axis=-1, keepdims=True)
    spread = jnp.mean(center * center, axis=-1, keepdims=True)
    inverse = lax.rsqrt(spread + NORM_EPSILON)
    return center * inverse, inverse


def gelu_parts(v):
    x = jnp.abs(v) * (2.0**-0.5)
    bell = jnp.exp(-x * x)
    t = 1.0 / (1.0 + 0.3275911 * x)
    series = t * (
        0.254829592
        + t * (-0.284496736 + t * (1.421413741 + t * (-1.453152027 + t * 1.061405429)))
    )
    tail = 0.5 * series * bell
    cumulative = jnp.where(v < 0.0, tail, 1.0 - tail)
    return cumulative, bell * (1.0 / math.sqrt(2.0 * math.pi))


class Place:
    def __init__(self):
        dp, tensor = lax.axis_index("dp"), lax.axis_index("tensor")
        self.z, self.x = lax.div(dp, 2), lax.rem(dp, 2)
        self.y, self.core = lax.div(tensor, 2), lax.rem(tensor, 2)
        self.tensor = tensor
        self.to_x = self.at(x=1 - self.x)
        self.to_y = self.at(y=1 - self.y)
        self.to_core = self.at(core=1 - self.core)
        self.to_corner = self.at(y=1 - self.y, core=1 - self.core)

    def at(self, z=None, x=None, y=None, core=None):
        z = self.z if z is None else z
        x = self.x if x is None else x
        y = self.y if y is None else y
        core = self.core if core is None else core
        return (z * 2 + x, y * 2 + core)

    def along(self, shift):
        return lax.rem(self.z + shift, 4)

    def near(self):
        return [
            (
                code,
                self.at(
                    x=lax.rem(self.x + code // 4, 2),
                    y=lax.rem(self.y + code // 2 % 2, 2),
                    core=lax.rem(self.core + code % 2, 2),
                ),
            )
            for code in range(1, 8)
        ]

    def greet(self, corner=False, near=False):
        peers = [self.at(z=self.along(shift)) for shift in (1, 2, 3)]
        if near:
            peers += [peer for _, peer in self.near()]
        else:
            peers += [self.to_x, self.to_y, self.to_core]
        if corner:
            peers.append(self.to_corner)
        barrier = pltpu.get_barrier_semaphore()
        for peer in peers:
            pl.semaphore_signal(barrier, inc=1, device_id=peer, device_id_type=MESH)
        pl.semaphore_wait(barrier, len(peers))


def remote(src, dst, send, recv, to):
    return pltpu.make_async_remote_copy(
        src_ref=src, dst_ref=dst, send_sem=send, recv_sem=recv, device_id=to, device_id_type=MESH
    )


def spread(steps, index, count):
    for place, step in enumerate(steps):
        pl.when(index == lax.div(place * count, len(steps)))(step)


class Gather:
    COUNT = 35

    @staticmethod
    def scratch(packs):
        return [
            pltpu.SemaphoreType.DMA((packs,)),
            pltpu.SemaphoreType.DMA((packs, Gather.COUNT)),
            pltpu.SemaphoreType.DMA((packs, Gather.COUNT)),
        ]

    @staticmethod
    def shapes(packs):
        return [jax.ShapeDtypeStruct((4, 4, 2) + pack.shape, pack.dtype) for pack in packs]

    def __init__(self, me, sources, outs, own_sem, send, recv):
        self.packs = [
            self.pack(me, source, out, own_sem.at[k], send.at[k], recv.at[k])
            for k, (source, out) in enumerate(zip(sources, outs))
        ]

    def pack(self, me, source, out, own_sem, send, recv):
        half = source.shape[0] // 2
        top, low = pl.ds(0, half), pl.ds(half, half)
        other = (1 - me.y) * 2 + me.core
        mine = out.at[me.tensor, me.z, me.x]

        def copy(slot, src, dst, to):
            return remote(src, dst, send.at[slot], recv.at[slot], to)

        parts = {"own": pltpu.make_async_copy(source, mine, own_sem)}
        for d in range(4):
            z = me.along(4 - d)
            block = out.at[me.tensor, z, me.x]
            origin = source if d == 0 else block
            if d > 0:
                parts["z", d] = copy(d - 1, source, mine, me.at(z=me.along(d)))
            parts["x", d] = copy(3 + d, origin, block, me.to_x)
            parts["y", d] = copy(7 + d, origin, block, me.to_y)
            parts["core", d] = copy(11 + d, origin, block, me.to_core)
            from_x, from_y = out.at[me.tensor, z, 1 - me.x], out.at[other, z, me.x]
            parts["xy", d] = copy(15 + d, from_x.at[top], from_x.at[top], me.to_y)
            parts["yx", d] = copy(19 + d, from_y.at[low], from_y.at[low], me.to_x)
            parts["core x", d] = copy(23 + d, from_x, from_x, me.to_core)
            parts["core y", d] = copy(27 + d, from_y, from_y, me.to_core)
            far = out.at[other, z, 1 - me.x]
            parts["core far", d] = copy(31 + d, far, far, me.to_core)
        return parts

    def begin(self):
        for parts in self.packs:
            for key in (("z", 1), ("x", 0), ("y", 0), ("core", 0), "own"):
                parts[key].start()

    def pass_on(self, d, following):
        for parts in self.packs:
            parts["z", d].wait()
            if following:
                parts["z", following].start()
            for way in ("x", "y", "core"):
                parts[way, d].start()

    def cross(self, d):
        for parts in self.packs:
            parts["x", d].wait_recv()
            parts["xy", d].start()
            parts["core x", d].start()
            parts["y", d].wait_recv()
            parts["yx", d].start()
            parts["core y", d].start()

    def far(self, d):
        for parts in self.packs:
            parts["xy", d].wait_recv()
            parts["yx", d].wait_recv()
            parts["core far", d].start()

    def end(self):
        for parts in self.packs:
            parts["own"].wait()
            for key, copy in parts.items():
                if key != "own" and key[0].startswith("core"):
                    copy.wait_recv()
            for key, copy in parts.items():
                if key != "own" and key[0] != "z":
                    copy.wait_send()

    def steps(self):
        return [
            functools.partial(self.pass_on, 1, 3),
            functools.partial(self.cross, 0),
            functools.partial(self.pass_on, 3, 2),
            functools.partial(self.cross, 1),
            functools.partial(self.far, 0),
            functools.partial(self.pass_on, 2, None),
            functools.partial(self.cross, 3),
            functools.partial(self.far, 1),
            functools.partial(self.cross, 2),
            functools.partial(self.far, 3),
            functools.partial(self.far, 2),
        ]


class Scatter:
    COUNT = 27

    @staticmethod
    def scratch(rows, cols):
        half = rows // 2
        return [
            pltpu.VMEM((4, 2, 2, rows, cols), BF16),
            pltpu.VMEM((2, 4, 2, rows, cols), BF16),
            pltpu.VMEM((4, 2, half, cols), BF16),
            pltpu.VMEM((4, 2, half, cols), BF16),
            pltpu.VMEM((4, half, cols), BF16),
            pltpu.VMEM((4, half, cols), BF16),
            pltpu.VMEM((3, rows, cols), BF16),
            pltpu.SemaphoreType.DMA((8,)),
            pltpu.SemaphoreType.DMA((Scatter.COUNT,)),
            pltpu.SemaphoreType.DMA((Scatter.COUNT,)),
        ]

    def __init__(
        self, me, source, out, total, from_core, from_x, from_y, turn_x, turn_y, from_z,
        load_sem, send, recv,
    ):
        self.me, self.out, self.total = me, out, total
        self.from_core, self.from_x, self.from_y = from_core, from_x, from_y
        self.turn_x, self.turn_y, self.from_z = turn_x, turn_y, from_z
        half = total.shape[3] // 2
        self.top, self.low = pl.ds(0, half), pl.ds(half, half)
        self.order = [me.along(d) for d in (2, 3, 1, 0)]
        self.parts = parts = {}

        def copy(slot, src, dst, to):
            return remote(src, dst, send.at[slot], recv.at[slot], to)

        for d, z in enumerate(self.order):
            for y in range(2):
                parts["load", d, y] = pltpu.make_async_copy(
                    source.at[2 * y + me.core, z], total.at[z, :, y], load_sem.at[2 * d + y]
                )
                parts["core", d, y] = copy(
                    2 * d + y, source.at[2 * y + 1 - me.core, z], from_core.at[y, z], me.to_core
                )
            parts["x", d] = copy(
                8 + d, total.at[z, 1 - me.x, :, self.top], from_x.at[z], me.to_x
            )
            parts["y", d] = copy(
                12 + d, total.at[z, :, 1 - me.y, self.low], from_y.at[z], me.to_y
            )
            parts["xy", d] = copy(
                16 + d, total.at[z, me.x, 1 - me.y, self.top], turn_y.at[z], me.to_y
            )
            parts["yx", d] = copy(
                20 + d, total.at[z, 1 - me.x, me.y, self.low], turn_x.at[z], me.to_x
            )
            if d < 3:
                parts["z", d] = copy(24 + d, total.at[z, me.x, me.y], from_z.at[d], me.at(z=z))

    def load(self, d):
        for y in range(2):
            self.parts["core", d, y].start()
            self.parts["load", d, y].start()

    def launch(self, d):
        self.parts["x", d].start()
        self.parts["y", d].start()

    def begin(self):
        self.load(0)
        self.load(1)

    def core(self, d):
        z = self.order[d]
        for y in range(2):
            self.parts["load", d, y].wait()
            self.parts["core", d, y].wait_recv()
            for x in range(2):
                self.total[z, x, y] += self.from_core[y, z, x]
        if d == 0:
            self.launch(0)
        if d < 2:
            self.load(d + 2)

    def cross(self, d):
        me, z = self.me, self.order[d]
        self.parts["x", d].wait_recv()
        self.parts["y", d].wait_recv()
        if d < 3:
            self.launch(d + 1)
        for y in range(2):
            self.total[z, me.x, y, self.top] += self.from_x[z, y]
        self.parts["xy", d].start()
        for x in range(2):
            self.total[z, x, me.y, self.low] += self.from_y[z, x]
        self.parts["yx", d].start()

    def far(self, d):
        me, z = self.me, self.order[d]
        self.parts["xy", d].wait_recv()
        self.total[z, me.x, me.y, self.top] += self.turn_y[z]
        self.parts["yx", d].wait_recv()
        self.total[z, me.x, me.y, self.low] += self.turn_x[z]
        if d < 3:
            self.parts["z", d].start()

    def end(self):
        me = self.me
        result = self.total[me.z, me.x, me.y].astype(F32)
        for d in range(3):
            self.parts["z", d].wait_recv()
            result = result + self.from_z[d].astype(F32)
        self.out[...] = result
        for key, copy in self.parts.items():
            if key[0] != "load":
                copy.wait_send()

    def steps(self):
        order = [
            (self.core, 0), (self.core, 1), (self.cross, 0), (self.core, 2), (self.cross, 1),
            (self.far, 0), (self.core, 3), (self.cross, 2), (self.far, 1), (self.cross, 3),
            (self.far, 2), (self.far, 3),
        ]
        return [functools.partial(step, d) for step, d in order]


def gather_kernel(packs, *refs):
    sources, small = refs[:packs], refs[packs]
    outs, small_out = refs[packs + 1 : 2 * packs + 1], refs[2 * packs + 1]
    sems, (small_own, small_send, small_recv) = refs[2 * packs + 2 : -3], refs[-3:]
    me = Place()
    gather = Gather(me, sources, outs, *sems)
    mine = small_out.at[me.x, me.z]
    own = pltpu.make_async_copy(small, mine, small_own)
    along = [
        remote(small, mine, small_send.at[d], small_recv.at[d], me.at(z=me.along(d)))
        for d in (1, 2, 3)
    ]
    row = small_out.at[me.x]
    across = remote(row, row, small_send.at[0], small_recv.at[0], me.to_x)
    me.greet()
    for copy in along + [own]:
        copy.start()
    gather.begin()
    own.wait()
    for copy in along:
        copy.wait_recv()
    across.start()
    for step in gather.steps():
        step()
    across.wait_recv()
    gather.end()
    for copy in along + [across]:
        copy.wait_send()


def gather_call(packs, small):
    count = len(packs)
    anywhere = pl.BlockSpec(memory_space=pl.ANY)
    outs = pl.pallas_call(
        functools.partial(gather_kernel, count),
        in_specs=[anywhere] * (count + 1),
        out_specs=[anywhere] * (count + 1),
        out_shape=Gather.shapes(packs)
        + [jax.ShapeDtypeStruct((2, 4) + small.shape, small.dtype)],
        scratch_shapes=Gather.scratch(count)
        + [
            pltpu.SemaphoreType.DMA,
            pltpu.SemaphoreType.DMA((4,)),
            pltpu.SemaphoreType.DMA((4,)),
        ],
        compiler_params=pltpu.CompilerParams(
            collective_id=3, has_side_effects=True, vmem_limit_bytes=ROOM
        ),
    )(*packs, small)
    return outs[:count], jnp.swapaxes(outs[count], 0, 1)


def tensor_barrier(count):
    me = lax.axis_index("tensor")
    barrier = pltpu.get_barrier_semaphore()
    for shift in range(1, count):
        pl.semaphore_signal(
            barrier, inc=1, device_id={"tensor": lax.rem(me + shift, count)}, device_id_type=MESH
        )
    pl.semaphore_wait(barrier, count - 1)


def share_kernel(count, mine_ref, out_ref, here_sem, send_sem, recv_sem):
    me = lax.axis_index("tensor")
    tensor_barrier(count)
    copies = []
    for shift in range(1, count):
        copies.append(
            pltpu.make_async_remote_copy(
                src_ref=mine_ref,
                dst_ref=out_ref.at[me],
                send_sem=send_sem.at[shift],
                recv_sem=recv_sem.at[shift],
                device_id={"tensor": lax.rem(me + shift, count)},
                device_id_type=MESH,
            )
        )
        copies[-1].start()
    own = pltpu.make_async_copy(mine_ref, out_ref.at[me], here_sem)
    own.start()
    own.wait()
    for copy in copies:
        copy.wait()


def share_call(mine, count):
    return pl.pallas_call(
        functools.partial(share_kernel, count),
        in_specs=[pl.BlockSpec(memory_space=pltpu.VMEM)],
        out_specs=pl.BlockSpec(memory_space=pltpu.VMEM),
        out_shape=jax.ShapeDtypeStruct((count,) + mine.shape, mine.dtype),
        scratch_shapes=[
            pltpu.SemaphoreType.DMA,
            pltpu.SemaphoreType.DMA((count,)),
            pltpu.SemaphoreType.DMA((count,)),
        ],
        compiler_params=pltpu.CompilerParams(collective_id=9, has_side_effects=True),
    )(mine)


def merge_kernel(count, parts_ref, out_ref, low, landed, send_sem, recv_sem):
    me = lax.axis_index("tensor")
    low[...] = parts_ref[...].astype(BF16)
    tensor_barrier(count)
    copies = []
    for shift in range(1, count):
        to = lax.rem(me + shift, count)
        copies.append(
            pltpu.make_async_remote_copy(
                src_ref=low.at[to],
                dst_ref=landed.at[shift],
                send_sem=send_sem.at[shift],
                recv_sem=recv_sem.at[shift],
                device_id={"tensor": to},
                device_id_type=MESH,
            )
        )
        copies[-1].start()
    total = parts_ref[me]
    for shift, copy in enumerate(copies, 1):
        copy.wait()
        total = total + landed[shift].astype(F32)
    out_ref[...] = total


def merge_call(parts):
    count = parts.shape[0]
    vmem = pl.BlockSpec(memory_space=pltpu.VMEM)
    return pl.pallas_call(
        functools.partial(merge_kernel, count),
        in_specs=[vmem],
        out_specs=vmem,
        out_shape=jax.ShapeDtypeStruct(parts.shape[1:], F32),
        scratch_shapes=[
            pltpu.VMEM(parts.shape, BF16),
            pltpu.VMEM(parts.shape, BF16),
            pltpu.SemaphoreType.DMA((count,)),
            pltpu.SemaphoreType.DMA((count,)),
        ],
        compiler_params=pltpu.CompilerParams(collective_id=10, has_side_effects=True),
    )(parts)


def blocks_of(parts):
    tens, width, cols = parts.shape
    return parts.reshape(tens, 4, 2, width // 8, cols)


def rotated(low, cos, sin):
    first, second = low[:HALF], low[HALF:ROT]
    return jnp.concatenate([first * cos - second * sin, second * cos + first * sin], axis=0)


def qkv_kernel(first, x_ref, norm_ref, trig_ref, qk_ref, *rest):
    if first:
        ov_ref, qt_ref, kv_ref, normed = rest
    else:
        qt_ref, normed = rest
    t = pl.program_id(0)

    @pl.when(t == 0)
    def _():
        x = x_ref[...].astype(F32)
        normed[...] = (standard(x)[0] * norm_ref[0:1] + norm_ref[1:2]).astype(BF16)

    cos, sin = trig_ref[0:HALF], trig_ref[HALF:ROT]
    lin = turn(dot(normed[...], qk_ref[0]))
    for head in range(HEADS_HERE):
        base = head * HD
        low = rotated(lin[base : base + ROT], cos, sin)
        qt_ref[0, base : base + ROT] = (low.astype(BF16).astype(F32) * SCALE).astype(BF16)
        qt_ref[0, base + ROT : base + HD] = (
            lin[base + ROT : base + HD].astype(BF16).astype(F32) * SCALE
        ).astype(BF16)
    qt_ref[0, QW:] = jnp.zeros_like(qt_ref[0, QW:])
    if first:

        @pl.when(t == 0)
        def _():
            value = turn(dot(normed[...], ov_ref[0]))[QW:]
            key = jnp.concatenate(
                [rotated(lin[QW : QW + ROT], cos, sin), lin[QW + ROT :]], axis=0
            )
            kv_ref[...] = turn(jnp.concatenate([key, value], axis=0)).astype(BF16)


def qkv_call(first, x, norms, trig, weights):
    rows, width = x.shape
    tens = weights.shape[0]
    whole = pl.BlockSpec(memory_space=pltpu.VMEM)
    in_specs = [whole, whole, whole, pl.BlockSpec((1, width, 256), lambda t: (t, 0, 0))]
    out_shape = [jax.ShapeDtypeStruct((tens, 256, rows), BF16)]
    out_specs = [pl.BlockSpec((1, 256, rows), lambda t: (t, 0, 0))]
    args = [x, norms, trig, weights]
    if first:
        in_specs.append(pl.BlockSpec((1, width, 256), lambda t: (0, 0, 1)))
        args.append(weights)
        out_shape.append(jax.ShapeDtypeStruct((rows, 2 * HD), BF16))
        out_specs.append(whole)
    return pl.pallas_call(
        functools.partial(qkv_kernel, first),
        grid=(tens,),
        in_specs=in_specs,
        out_specs=out_specs,
        out_shape=out_shape,
        scratch_shapes=[pltpu.VMEM((rows, width), BF16)],
        compiler_params=pltpu.CompilerParams(vmem_limit_bytes=ROOM),
    )(*args)


class Refs:
    def __init__(self, refs):
        self.refs = list(refs)

    def take(self, count):
        taken, self.refs = self.refs[:count], self.refs[count:]
        return taken


def attend_kernel(share, packs, *refs):
    refs = Refs(refs)
    qt_ref, kv_ref = refs.take(2)
    sources = refs.take(packs)
    at_ref, lse_ref = refs.take(2)
    all_ref = refs.take(1)[0] if share else None
    outs = refs.take(packs)
    keys, values_t = refs.take(2)
    steps = []
    if packs:
        me = Place()
        gather = Gather(me, sources, outs, *refs.take(3))
        steps = gather.steps()
    t = pl.program_id(0)
    tens = pl.num_programs(0)
    rows = qt_ref.shape[2]
    place = lax.axis_index("tensor")
    count = tens * (place + 1)
    if share:
        landed, send, recv = refs.take(3)
        peers = (me.to_core, me.to_y, me.to_corner)
        copies = [
            remote(kv_ref, landed.at[place], send.at[k], recv.at[k], peer)
            for k, peer in enumerate(peers)
        ]

    @pl.when(t == 0)
    def _():
        if packs:
            me.greet(corner=share)
        if share:
            for copy in copies:
                copy.start()
        if packs:
            gather.begin()
        if share:
            here = pl.ds(pl.multiple_of(place * rows, rows), rows)
            landed[place] = kv_ref[...]
            keys[here, :] = kv_ref[:, :HD]
            values_t[:, here] = turn(kv_ref[...])[HD:].astype(BF16)
        else:
            keys[...] = kv_ref[:, :HD]
            values_t[...] = turn(kv_ref[...])[HD:].astype(BF16)

    def block(index, carry, diagonal):
        here = pl.ds(pl.multiple_of(index * rows, rows), rows)
        key = keys[here, :]
        value_t = values_t[:, here]
        out = []
        for head in range(HEADS_HERE):
            scores = dot(key, qt_ref[0, head * HD : (head + 1) * HD])
            if diagonal:
                below = lax.broadcasted_iota(jnp.int32, scores.shape, 0)
                across = lax.broadcasted_iota(jnp.int32, scores.shape, 1)
                scores = jnp.where(below <= across, scores, -1e30)
            peak = jnp.max(scores, axis=0, keepdims=True)
            if carry is not None:
                peak = jnp.maximum(peak, carry[head][0])
            weights = jnp.exp(scores - peak)
            total = jnp.sum(weights, axis=0, keepdims=True)
            mixed = dot(value_t, weights.astype(BF16))
            if carry is not None:
                fade = jnp.exp(carry[head][0] - peak)
                total = total + carry[head][1] * fade
                mixed = mixed + carry[head][2] * fade
            out.append((peak, total, mixed))
        return tuple(out)

    spread(steps, t * (place + 1), count)
    carry = block(place, None, True)
    if share:

        @pl.when(t == 0)
        def _():
            for copy in copies:
                copy.wait()
            for part in range(landed.shape[0]):
                here = pl.ds(part * rows, rows)
                keys[here, :] = landed[part, :, :HD]
                values_t[:, here] = turn(landed[part])[HD:].astype(BF16)
            all_ref[...] = landed[...]

    def later(i, carry):
        spread(steps, t * (place + 1) + 1 + i, count)
        return block(i, carry, False)

    carry = lax.fori_loop(0, place, later, carry)
    lse_ref[...] = jnp.zeros_like(lse_ref)
    for head in range(HEADS_HERE):
        peak, total, mixed = carry[head]
        at_ref[0, head * HD : (head + 1) * HD] = (mixed / total).astype(BF16)
        lse_ref[0, head : head + 1] = peak + jnp.log(total)
    at_ref[0, QW:] = jnp.zeros_like(at_ref[0, QW:])
    if packs:
        pl.when(t == tens - 1)(gather.end)


def comm_params(ident):
    if ident is None:
        return pltpu.CompilerParams(vmem_limit_bytes=ROOM)
    return pltpu.CompilerParams(
        collective_id=ident, has_side_effects=True, vmem_limit_bytes=ROOM
    )


def attend_call(qt, kv, length, packs=(), share=False, ident=None):
    tens, _, rows = qt.shape
    whole = pl.BlockSpec(memory_space=pltpu.VMEM)
    anywhere = pl.BlockSpec(memory_space=pl.ANY)
    part = pl.BlockSpec((1, 256, rows), lambda t: (t, 0, 0))
    out_specs = [part, pl.BlockSpec((1, 8, rows), lambda t: (t, 0, 0))]
    out_shape = [
        jax.ShapeDtypeStruct((tens, 256, rows), BF16),
        jax.ShapeDtypeStruct((tens, 8, rows), F32),
    ]
    scratch = [pltpu.VMEM((length, HD), BF16), pltpu.VMEM((HD, length), BF16)]
    if packs:
        scratch += Gather.scratch(len(packs))
    if share:
        out_specs.append(whole)
        out_shape.append(jax.ShapeDtypeStruct((tens,) + kv.shape, BF16))
        scratch += [
            pltpu.VMEM((tens,) + kv.shape, BF16),
            pltpu.SemaphoreType.DMA((3,)),
            pltpu.SemaphoreType.DMA((3,)),
        ]
    out_specs += [anywhere] * len(packs)
    out_shape += Gather.shapes(packs) if packs else []
    return pl.pallas_call(
        functools.partial(attend_kernel, share, len(packs)),
        grid=(tens,),
        in_specs=[part, whole] + [anywhere] * len(packs),
        out_specs=out_specs,
        out_shape=out_shape,
        scratch_shapes=scratch,
        compiler_params=comm_params(ident),
    )(qt, kv, *packs)


def mix_kernel(packs, *refs):
    refs = Refs(refs)
    x_ref, norm_ref, at_ref, o_ref, up_ref, down_ref = refs.take(6)
    sources = refs.take(packs)
    out_ref, act_ref, slope_ref = refs.take(3)
    outs = refs.take(packs)
    normed, total = refs.take(2)
    t = pl.program_id(0)
    tens = pl.num_programs(0)
    steps = []
    if packs:
        me = Place()
        gather = Gather(me, sources, outs, *refs.take(3))
        steps = gather.steps()

    @pl.when(t == 0)
    def _():
        if packs:
            me.greet()
            gather.begin()
        x = x_ref[...].astype(F32)
        normed[...] = (standard(x)[0] * norm_ref[2:3] + norm_ref[3:4]).astype(BF16)
        total[...] = x

    attended = turn(at_ref[0, :QW]).astype(BF16)
    step = 256
    parts = up_ref.shape[2] // step
    for part in range(parts):
        spread(steps, t * (parts + 1) + part, tens * (parts + 1))
        cols = pl.ds(part * step, step)
        pre = dot(normed[...], up_ref[0, :, cols])
        cumulative, bell = gelu_parts(pre)
        act_ref[0, :, cols] = (pre * cumulative).astype(BF16)
        slope_ref[0, :, cols] = (cumulative + pre * bell).astype(BF16)
    spread(steps, t * (parts + 1) + parts, tens * (parts + 1))
    total[...] += dot_nt(attended, o_ref[0, :, :QW]) + dot_nt(act_ref[0], down_ref[0])

    @pl.when(t == tens - 1)
    def _():
        out_ref[...] = total[...]
        if packs:
            gather.end()


def mix_call(x, norms, at, outward, feed, packs=(), ident=None):
    rows, width = x.shape
    tens = feed.shape[0]
    hidden = feed.shape[2] // 2
    whole = pl.BlockSpec(memory_space=pltpu.VMEM)
    anywhere = pl.BlockSpec(memory_space=pl.ANY)
    wide = pl.BlockSpec((1, rows, hidden), lambda t: (t, 0, 0))
    return pl.pallas_call(
        functools.partial(mix_kernel, len(packs)),
        grid=(tens,),
        in_specs=[
            whole,
            whole,
            pl.BlockSpec((1, 256, rows), lambda t: (t, 0, 0)),
            pl.BlockSpec((1, width, 256), lambda t: (t, 0, 1)),
            pl.BlockSpec((1, width, hidden), lambda t: (t, 0, 0)),
            pl.BlockSpec((1, width, hidden), lambda t: (t, 0, 1)),
        ]
        + [anywhere] * len(packs),
        out_specs=[whole, wide, wide] + [anywhere] * len(packs),
        out_shape=[
            jax.ShapeDtypeStruct((rows, width), F32),
            jax.ShapeDtypeStruct((tens, rows, hidden), BF16),
            jax.ShapeDtypeStruct((tens, rows, hidden), BF16),
        ]
        + (Gather.shapes(packs) if packs else []),
        scratch_shapes=[pltpu.VMEM((rows, width), BF16), pltpu.VMEM((rows, width), F32)]
        + (Gather.scratch(len(packs)) if packs else []),
        compiler_params=comm_params(ident),
    )(x, norms, at, outward, feed, feed, *packs)


def mix_back_kernel(sends, *refs):
    refs = Refs(refs)
    gx_ref, x_ref, norm_ref, at_ref, act_ref, slope_ref, o_ref, up_ref, down_ref = refs.take(9)
    sent = refs.take(sends)
    pack_ref, dot_ref, mlp_ref = refs.take(3)
    summed = refs.take(sends)
    low, low_t, normed_t = refs.take(3)
    t = pl.program_id(0)
    tens = pl.num_programs(0)
    steps = []
    if sends:
        me = Place()
        scatter = Scatter(me, sent[0], summed[0], *refs.take(10))
        steps = scatter.steps()

    @pl.when(t == 0)
    def _():
        if sends:
            me.greet()
            scatter.begin()
        grad = gx_ref[...].astype(BF16)
        low[...] = grad
        low_t[...] = turn(grad).astype(BF16)
        x = x_ref[...].astype(F32)
        normed = (standard(x)[0] * norm_ref[2:3] + norm_ref[3:4]).astype(BF16)
        normed_t[...] = turn(normed).astype(BF16)
        mlp_ref[...] = jnp.zeros_like(mlp_ref)

    def poll(part):
        spread(steps, t * 4 + part, tens * 4)

    hidden = up_ref.shape[2]
    poll(0)
    grad_attended = dot(low[...], o_ref[0, :, :QW])
    dot_ref[0, :QW] = turn(grad_attended).astype(BF16)
    dot_ref[0, QW:] = jnp.zeros_like(dot_ref[0, QW:])
    pack_ref[0, :, 2 * hidden :] = dot_nt(low_t[...], at_ref[0]).astype(BF16)
    poll(1)
    pack_ref[0, :, hidden : 2 * hidden] = dot(low_t[...], act_ref[0]).astype(BF16)
    poll(2)
    grad_pre = (dot(low[...], down_ref[0]) * slope_ref[0].astype(F32)).astype(BF16)
    poll(3)
    pack_ref[0, :, :hidden] = dot(normed_t[...], grad_pre).astype(BF16)
    mlp_ref[...] += dot_nt(grad_pre, up_ref[0])
    if sends:
        pl.when(t == tens - 1)(scatter.end)


def mix_back_call(gx, x, norms, at, act, slope, outward, feed, sent=None, ident=None):
    rows, width = x.shape
    tens = feed.shape[0]
    hidden = act.shape[2]
    whole = pl.BlockSpec(memory_space=pltpu.VMEM)
    wide = pl.BlockSpec((1, rows, hidden), lambda t: (t, 0, 0))
    part = pl.BlockSpec((1, 256, rows), lambda t: (t, 0, 0))
    args = [gx, x, norms, at, act, slope, outward, feed, feed]
    in_specs = [
        whole,
        whole,
        whole,
        part,
        wide,
        wide,
        pl.BlockSpec((1, width, 256), lambda t: (t, 0, 1)),
        pl.BlockSpec((1, width, hidden), lambda t: (t, 0, 0)),
        pl.BlockSpec((1, width, hidden), lambda t: (t, 0, 1)),
    ]
    out_specs = [pl.BlockSpec((1, width, 2 * hidden + 256), lambda t: (t, 0, 0)), part, whole]
    out_shape = [
        jax.ShapeDtypeStruct((tens, width, 2 * hidden + 256), BF16),
        jax.ShapeDtypeStruct((tens, 256, rows), BF16),
        jax.ShapeDtypeStruct((rows, width), F32),
    ]
    scratch = [
        pltpu.VMEM((rows, width), BF16),
        pltpu.VMEM((width, rows), BF16),
        pltpu.VMEM((width, rows), BF16),
    ]
    if sent is not None:
        sent = blocks_of(sent)
        args.append(sent)
        in_specs.append(pl.BlockSpec(memory_space=pl.ANY))
        out_specs.append(whole)
        out_shape.append(jax.ShapeDtypeStruct(sent.shape[3:], F32))
        scratch += Scatter.scratch(*sent.shape[3:])
    return pl.pallas_call(
        functools.partial(mix_back_kernel, int(sent is not None)),
        grid=(tens,),
        in_specs=in_specs,
        out_specs=out_specs,
        out_shape=out_shape,
        scratch_shapes=scratch,
        compiler_params=comm_params(ident),
    )(*args)


def attend_back_kernel(start_given, sends, merge, *refs):
    refs = Refs(refs)
    qt_ref, dot_ref, at_ref, lse_ref, kv_ref, trig_ref = refs.take(6)
    before_ref = refs.take(1)[0] if start_given else None
    sent = refs.take(sends)
    gqt_ref, dkv_ref = refs.take(2)
    summed = refs.take(sends)
    keys, values, keys_t, dkeys, dvalues = refs.take(5)
    t = pl.program_id(0)
    tens = pl.num_programs(0)
    rows = qt_ref.shape[2]
    parts = kv_ref.shape[0] // rows
    place = lax.axis_index("tensor")
    count = tens * (place + 1)
    steps = []
    if sends:
        me = Place()
        scatter = Scatter(me, sent[0], summed[0], *refs.take(10))
        steps = scatter.steps()
    if merge:
        low, landed, send, recv = refs.take(4)
        peers = (me.to_core, me.to_y, me.to_corner)
        copies = [
            remote(low.at[peer[1]], landed.at[k], send.at[k], recv.at[k], peer)
            for k, peer in enumerate(peers)
        ]

    @pl.when(t == 0)
    def _():
        if sends:
            me.greet(corner=merge)
            scatter.begin()
        both_t = turn(kv_ref[...])
        keys[...] = kv_ref[:, :HD]
        keys_t[...] = both_t[:HD].astype(BF16)
        values[...] = turn(both_t[HD:]).astype(BF16)
        dkeys[...] = jnp.zeros_like(dkeys)
        dvalues[...] = jnp.zeros_like(dvalues)

    inner = []
    for head in range(HEADS_HERE):
        span = slice(head * HD, (head + 1) * HD)
        inner.append(
            jnp.sum(
                dot_ref[0, span].astype(F32) * at_ref[0, span].astype(F32), axis=0, keepdims=True
            )
        )

    def block(index, carry, diagonal):
        here = pl.ds(pl.multiple_of(index * rows, rows), rows)
        key = keys[here, :]
        value = values[here, :]
        key_t = keys_t[:, here]
        out = []
        dkey = None
        for head in range(HEADS_HERE):
            span = slice(head * HD, (head + 1) * HD)
            query_t = qt_ref[0, span]
            grad_t = dot_ref[0, span]
            scores = dot(key, query_t)
            probs = jnp.exp(scores - lse_ref[0, head : head + 1])
            if diagonal:
                below = lax.broadcasted_iota(jnp.int32, scores.shape, 0)
                across = lax.broadcasted_iota(jnp.int32, scores.shape, 1)
                probs = jnp.where(below <= across, probs, 0.0)
            grad_probs = dot(value, grad_t)
            grad_scores = (probs * (grad_probs - inner[head])).astype(BF16)
            part_v = dot_nt(probs.astype(BF16), grad_t)
            part_k = dot_nt(grad_scores, query_t)
            dkey = part_k if dkey is None else dkey + part_k
            dvalue = part_v if head == 0 else dvalue + part_v
            part_q = dot(key_t, grad_scores)
            out.append(part_q if carry is None else carry[head] + part_q)
        dkeys[here, :] += dkey
        dvalues[here, :] += dvalue
        return tuple(out)

    def later(i, carry):
        spread(steps, t * (place + 1) + 1 + i, count)
        return block(i, carry, False)

    spread(steps, t * (place + 1), count)
    carry = block(place, None, True)
    carry = lax.fori_loop(0, place, later, carry)
    cos, sin = trig_ref[0:HALF], trig_ref[HALF:ROT]
    for head in range(HEADS_HERE):
        base = head * HD
        grad = carry[head] * SCALE
        gqt_ref[0, base : base + ROT] = rotated(grad[:ROT], cos, -sin).astype(BF16)
        gqt_ref[0, base + ROT : base + HD] = grad[ROT:].astype(BF16)
    gqt_ref[0, QW:] = jnp.zeros_like(gqt_ref[0, QW:])

    @pl.when(t == tens - 1)
    def _():
        both = jnp.concatenate([turn(dkeys[...]), turn(dvalues[...])], axis=0)
        for part in range(parts):
            piece = both[:, part * rows : (part + 1) * rows]
            if start_given:
                piece = piece + before_ref[part]
            if not merge:
                dkv_ref[part] = piece
            else:
                low[part] = piece.astype(BF16)

                @pl.when(place == part)
                def _(piece=piece):
                    dkv_ref[...] = piece

        if merge:
            for copy in copies:
                copy.start()
        if sends:
            scatter.end()
        if merge:
            for copy in copies:
                copy.wait_recv()
            dkv_ref[...] += (
                landed[0].astype(F32) + landed[1].astype(F32) + landed[2].astype(F32)
            )
            for copy in copies:
                copy.wait_send()


def attend_back_call(
    qt, dout, at, lse, kv, trig, before=None, sent=None, merge=False, ident=None
):
    tens, _, rows = qt.shape
    length = kv.shape[0]
    whole = pl.BlockSpec(memory_space=pltpu.VMEM)
    part = pl.BlockSpec((1, 256, rows), lambda t: (t, 0, 0))
    args = [qt, dout, at, lse, kv, trig]
    in_specs = [part, part, part, pl.BlockSpec((1, 8, rows), lambda t: (t, 0, 0)), whole, whole]
    pieces = (length // rows, 2 * HD, rows)
    out_specs = [part, whole]
    out_shape = [
        jax.ShapeDtypeStruct((tens, 256, rows), BF16),
        jax.ShapeDtypeStruct(pieces[1:] if merge else pieces, F32),
    ]
    scratch = [
        pltpu.VMEM((length, HD), BF16),
        pltpu.VMEM((length, HD), BF16),
        pltpu.VMEM((HD, length), BF16),
        pltpu.VMEM((length, HD), F32),
        pltpu.VMEM((length, HD), F32),
    ]
    if before is not None:
        args.append(before)
        in_specs.append(whole)
    if sent is not None:
        sent = blocks_of(sent)
        args.append(sent)
        in_specs.append(pl.BlockSpec(memory_space=pl.ANY))
        out_specs.append(whole)
        out_shape.append(jax.ShapeDtypeStruct(sent.shape[3:], F32))
        scratch += Scatter.scratch(*sent.shape[3:])
    if merge:
        scratch += [
            pltpu.VMEM(pieces, BF16),
            pltpu.VMEM((3,) + pieces[1:], BF16),
            pltpu.SemaphoreType.DMA((3,)),
            pltpu.SemaphoreType.DMA((3,)),
        ]
    return pl.pallas_call(
        functools.partial(attend_back_kernel, before is not None, int(sent is not None), merge),
        grid=(tens,),
        in_specs=in_specs,
        out_specs=out_specs,
        out_shape=out_shape,
        scratch_shapes=scratch,
        compiler_params=comm_params(ident),
    )(*args)


def norm_back_kernel(first, gx_ref, x_ref, norm_ref, mlp_ref, gqt_ref, qk_ref, *rest):
    if first:
        ov_ref, dkv_ref, trig_ref, other_ref, out_ref, pack_ref, normed_t, attn, shared = rest
    else:
        out_ref, pack_ref, sums_ref, normed_t, attn = rest
    t = pl.program_id(0)

    @pl.when(t == 0)
    def _():
        x = x_ref[...].astype(F32)
        normed = (standard(x)[0] * norm_ref[0:1] + norm_ref[1:2]).astype(BF16)
        normed_t[...] = turn(normed).astype(BF16)
        if first:
            cos, sin = trig_ref[0:HALF], trig_ref[HALF:ROT]
            grad = dkv_ref[...]
            shared[:ROT] = rotated(grad[:ROT], cos, -sin).astype(BF16)
            shared[ROT:] = grad[ROT:].astype(BF16)
            attn[...] = dot_nt(turn(shared[:HD]).astype(BF16), qk_ref[0, :, QW:]) + dot_nt(
                turn(shared[HD:]).astype(BF16), ov_ref[0, :, QW:]
            )
        else:
            attn[...] = jnp.zeros_like(attn)

    grad_t = gqt_ref[0, :QW]
    attn[...] += dot_nt(turn(grad_t).astype(BF16), qk_ref[0, :, :QW])
    if first:
        left = jnp.concatenate([grad_t, shared[:HD]], axis=0)
        pack_ref[t, :, :256] = dot_nt(normed_t[...], left).astype(BF16)
    else:
        pack_ref[0] = dot_nt(normed_t[...], gqt_ref[0]).astype(BF16)

    @pl.when(t == pl.num_programs(0) - 1)
    def _():
        unit, inverse = standard(x_ref[...].astype(F32))
        attn_grad, mlp_grad = attn[...], mlp_ref[...]
        sums = jnp.concatenate(
            [
                jnp.sum(attn_grad * unit, axis=0, keepdims=True),
                jnp.sum(attn_grad, axis=0, keepdims=True),
                jnp.sum(mlp_grad * unit, axis=0, keepdims=True),
                jnp.sum(mlp_grad, axis=0, keepdims=True),
            ],
            axis=0,
        )
        if first:
            pad = jnp.zeros((HD, sums.shape[1]), F32)
            lower = turn(jnp.concatenate([pad, sums, other_ref[...], pad[8:]], axis=0))
            upper = jnp.concatenate([shared[HD:], jnp.zeros_like(shared[HD:])], axis=0)
            right = (dot_nt(normed_t[...], upper) + lower).astype(BF16)
            for part in range(pack_ref.shape[0]):
                pack_ref[part, :, 256:] = right
        else:
            sums_ref[...] = sums
        grad = attn_grad * norm_ref[0:1] + mlp_grad * norm_ref[2:3]
        mean = jnp.mean(grad, axis=-1, keepdims=True)
        slant = jnp.mean(grad * unit, axis=-1, keepdims=True)
        out_ref[...] = gx_ref[...] + inverse * (grad - mean - unit * slant)


def norm_back_call(first, gx, x, norms, mlp, gqt, weights, dkv=None, trig=None, other=None):
    rows, width = x.shape
    tens = weights.shape[0]
    whole = pl.BlockSpec(memory_space=pltpu.VMEM)
    part = pl.BlockSpec((1, 256, rows), lambda t: (t, 0, 0))
    args = [gx, x, norms, mlp, gqt, weights]
    in_specs = [whole] * 4 + [part, pl.BlockSpec((1, width, 256), lambda t: (t, 0, 0))]
    scratch = [pltpu.VMEM((width, rows), BF16), pltpu.VMEM((rows, width), F32)]
    out_shape = [jax.ShapeDtypeStruct((rows, width), F32)]
    if first:
        args += [weights, dkv, trig, other]
        in_specs += [pl.BlockSpec((1, width, 256), lambda t: (0, 0, 1)), whole, whole, whole]
        scratch.append(pltpu.VMEM((2 * HD, rows), BF16))
        out_shape.append(jax.ShapeDtypeStruct((tens, width, 384), BF16))
        out_specs = [whole, whole]
    else:
        out_shape.append(jax.ShapeDtypeStruct((tens, width, 256), BF16))
        out_shape.append(jax.ShapeDtypeStruct((4, width), F32))
        out_specs = [whole, pl.BlockSpec((1, width, 256), lambda t: (t, 0, 0)), whole]
    return pl.pallas_call(
        functools.partial(norm_back_kernel, first),
        grid=(tens,),
        in_specs=in_specs,
        out_specs=out_specs,
        out_shape=out_shape,
        scratch_shapes=scratch,
        compiler_params=comm_params(None),
    )(*args)


def lamb_parts(weight, first, second, grad):
    first_new = BETA_FIRST * first + (1.0 - BETA_FIRST) * grad
    second_new = BETA_SECOND * second + (1.0 - BETA_SECOND) * grad * grad
    update = (
        first_new
        / (1.0 - BETA_FIRST**STEP)
        / (jnp.sqrt(second_new / (1.0 - BETA_SECOND**STEP)) + ADAM_EPSILON)
        + WEIGHT_DECAY * weight
    )
    return (first_new, second_new, update)


def keyval_grad(late):
    lane = lax.broadcasted_iota(jnp.int32, (late.shape[0], 2 * HD), 1)
    left = pltpu.roll(late[:, 128:256], HD, 1)
    right = pltpu.roll(late[:, 256:384], HD, 1)
    return jnp.where(lane < HD, left, right)


def norm_grad(late):
    return turn(late[:, 256:384])[HD : HD + 8]


def square(value):
    total = jnp.sum(value * value, axis=1, keepdims=True)
    return jnp.sum(total, axis=0, keepdims=True)


def lanes(pairs):
    lane = lax.broadcasted_iota(jnp.int32, (1, 128), 1)
    row = jnp.zeros((1, 128), F32)
    for place, value in pairs:
        row = jnp.where(lane == place, value, row)
    return row


class Tensors:
    def __init__(self, refs, early, late):
        self.refs = refs
        self.early, self.late = early, late

    def early_grad(self, layer, which):
        pack = self.early[layer]
        hidden = (pack.shape[1] - 256) // 2
        if which == "up":
            return pack[:, :hidden]
        if which == "down":
            return turn(pack[:, hidden : 2 * hidden])
        return turn(pack[:, 2 * hidden :])[:QW]

    def parts(self, array, index, grad):
        weight, first, second = (ref[...] if index is None else ref[index] for ref in array)
        return (weight,) + lamb_parts(weight, first, second, grad)

    def each(self, late0):
        query, keyval, output, upward, downward, norms = range(6)
        for layer in range(2):
            yield 5 + layer, upward, layer, lambda: self.early_grad(layer, "up")
            yield 7 + layer, downward, layer, lambda: self.early_grad(layer, "down")
            yield 3 + layer, output, layer, lambda: self.early_grad(layer, "output")
        yield 1, query, 1, lambda: self.late[1][:, :QW]
        yield 0, query, 0, lambda: late0()[:, :QW]
        yield 2, keyval, None, lambda: keyval_grad(late0())
        for layer in range(2):
            yield 9 + 4 * layer, norms, layer, lambda: norm_grad(late0())[4 * layer : 4 * layer + 4]


def norms_kernel(*refs):
    refs = Refs(refs)
    parts_ref, early0, early1, late1 = refs.take(4)
    arrays = [refs.take(3) for _ in range(6)]
    late0_ref, sums_ref = refs.take(2)
    scatter_refs = refs.take(10)
    near_land, along_land, send, recv = refs.take(4)
    me = Place()
    scatter = Scatter(me, parts_ref, late0_ref, *scatter_refs)
    steps = scatter.steps()
    me.greet(near=True)
    scatter.begin()
    tensors = Tensors(arrays, (early0, early1), (None, late1))
    leader = (me.tensor == 0).astype(F32)
    old, new = [], []

    def late0():
        return late0_ref[...]

    waiting = list(steps)
    for place, array, index, grad in tensors.each(late0):
        if place == 0:
            for step in waiting:
                step()
            scatter.end()
        elif place != 2 and place < 9 and place != 1 and waiting:
            waiting.pop(0)()
            waiting.pop(0)()
        weight, _, _, update = tensors.parts(arrays[array], index, grad())
        if place >= 9:
            for row in range(4):
                old.append((place + row, square(weight[row : row + 1]) * leader))
                new.append((place + row, square(update[row : row + 1]) * leader))
        else:
            scale = leader if place == 2 else 1.0
            old.append((place, square(weight) * scale))
            new.append((place, square(update) * scale))

    near_land[0] = jnp.concatenate([lanes(old), lanes(new), jnp.zeros((6, 128), F32)], axis=0)
    copies = []
    for code, peer in me.near():
        copies.append(
            remote(near_land.at[0], near_land.at[code], send.at[code], recv.at[code], peer)
        )
        copies[-1].start()
    for copy in copies:
        copy.wait()
    total = jnp.zeros((8, 128), F32)
    for x in range(2):
        for y in range(2):
            for core in range(2):
                code = lax.rem(x + me.x, 2) * 4 + lax.rem(y + me.y, 2) * 2
                total = total + near_land[code + lax.rem(core + me.core, 2)]
    along_land[0] = total
    copies = []
    for shift in (1, 2, 3):
        copies.append(
            remote(
                along_land.at[0], along_land.at[shift], send.at[7 + shift],
                recv.at[7 + shift], me.at(z=me.along(shift)),
            )
        )
        copies[-1].start()
    for copy in copies:
        copy.wait()
    total = jnp.zeros((8, 128), F32)
    for z in range(4):
        total = total + along_land[me.along(4 - z)]
    sums_ref[...] = total


def norms_call(parts, early, late1, arrays):
    parts = blocks_of(parts)
    rows, cols = parts.shape[3:]
    vmem = pl.BlockSpec(memory_space=pltpu.VMEM)
    flat = [ref for array in arrays for ref in array]
    return pl.pallas_call(
        norms_kernel,
        in_specs=[pl.BlockSpec(memory_space=pl.ANY)] + [vmem] * (3 + len(flat)),
        out_specs=[vmem, vmem],
        out_shape=[
            jax.ShapeDtypeStruct((rows, cols), F32),
            jax.ShapeDtypeStruct((8, 128), F32),
        ],
        scratch_shapes=Scatter.scratch(rows, cols)
        + [
            pltpu.VMEM((8, 8, 128), F32),
            pltpu.VMEM((4, 8, 128), F32),
            pltpu.SemaphoreType.DMA((11,)),
            pltpu.SemaphoreType.DMA((11,)),
        ],
        compiler_params=comm_params(8),
    )(parts, *early, late1, *flat)


def lamb_kernel(*refs):
    refs = Refs(refs)
    sums_ref, early0, early1, late0_ref, late1 = refs.take(5)
    arrays = [refs.take(3) for _ in range(6)]
    outs = [refs.take(4) for _ in range(6)]
    norm_out, ratio_out = refs.take(2)
    weight_norm = jnp.sqrt(sums_ref[0:1])
    update_norms = jnp.sqrt(sums_ref[1:2])
    used = lax.broadcasted_iota(jnp.int32, (1, 128), 1) < 17
    ratios = jnp.where(used, weight_norm / jnp.where(used, update_norms, 1.0), 0.0)
    norm_out[...] = update_norms
    ratio_out[...] = ratios
    tensors = Tensors(arrays, (early0, early1), (None, late1))
    for place, array, index, grad in tensors.each(lambda: late0_ref[...]):
        weight, first, second, update = tensors.parts(arrays[array], index, grad())
        if place >= 9:
            factor = jnp.concatenate(
                [ratios[:, place + row : place + row + 1] for row in range(4)], axis=0
            )
        else:
            factor = ratios[:, place : place + 1]
        after = weight - LEARN_RATE * factor * update
        where = Ellipsis if index is None else index
        for ref, value in zip(outs[array], (first, second, after, after.astype(BF16))):
            ref[where] = value


def lamb_call(sums, early, late, arrays):
    vmem = pl.BlockSpec(memory_space=pltpu.VMEM)
    flat = [ref for array in arrays for ref in array]
    shapes = []
    for array in arrays:
        shape = array[0].shape
        shapes += [jax.ShapeDtypeStruct(shape, F32)] * 3 + [jax.ShapeDtypeStruct(shape, BF16)]
    shapes += [jax.ShapeDtypeStruct((1, 128), F32)] * 2
    return pl.pallas_call(
        lamb_kernel,
        in_specs=[vmem] * (5 + len(flat)),
        out_specs=[vmem] * len(shapes),
        out_shape=shapes,
        compiler_params=comm_params(None),
    )(sums, *early, *late, *flat)


def angles(places):
    steps = jnp.arange(HALF).astype(F32)
    inverse = jnp.exp(steps * (-2.0 * math.log(10000.0) / ROT))
    phase = (0.25 * inverse)[:, None] * places.astype(F32)[None, :]
    return jnp.concatenate([jnp.cos(phase), jnp.sin(phase)], axis=0)


def param_squares(arrays, leader):
    query, keyval, output, upward, downward, norms = arrays
    return jnp.concatenate(
        [
            jnp.sum(query * query, axis=(1, 2)),
            (jnp.sum(keyval * keyval) * leader)[None],
            jnp.sum(output * output, axis=(1, 2)),
            jnp.sum(upward * upward, axis=(1, 2)),
            jnp.sum(downward * downward, axis=(1, 2)),
            jnp.sum(norms * norms, axis=2).reshape(8) * leader,
        ]
    )


def apply_trust(masters, updates, trust):
    factors = (
        trust[0:2][:, None, None],
        trust[2],
        trust[3:5][:, None, None],
        trust[5:7][:, None, None],
        trust[7:9][:, None, None],
        trust[9:17].reshape(2, 4, 1),
    )
    return tuple(
        (
            weight - LEARN_RATE * factor * update
            for weight, factor, update in zip(masters, factors, updates)
        )
    )


def plain_scatter(parts, depth):
    pieces = parts.reshape(-1, depth, parts.shape[-1])
    return lax.psum_scatter(pieces, ("tensor", "dp"), scatter_dimension=0).astype(F32)


def shards(
    fast,
    hidden_in,
    out_grad,
    positions,
    query_weight,
    keyval_weight,
    output_weight,
    up_weight,
    down_weight,
    norm_params,
    query_first,
    query_second,
    keyval_first,
    keyval_second,
    output_first,
    output_second,
    up_first,
    up_second,
    down_first,
    down_second,
    norm_first,
    norm_second,
):
    masters = (query_weight, keyval_weight, output_weight, up_weight, down_weight, norm_params)
    tensor = lax.axis_index("tensor")
    leader = (tensor == 0).astype(F32)
    rows, width = hidden_in.shape
    tens = positions.shape[0] // rows
    depth = keyval_weight.shape[0]

    narrow, wide = [], []
    for layer in range(2):
        if layer == 0:
            keys, values = keyval_weight[:, :HD], keyval_weight[:, HD:]
        else:
            keys = values = jnp.zeros((depth, HD), F32)
        pieces = [query_weight[layer], keys, output_weight[layer].T, values]
        narrow.append(jnp.concatenate(pieces, axis=1).astype(BF16))
        wide.append(
            jnp.concatenate([up_weight[layer], down_weight[layer].T], axis=1).astype(BF16)
        )
    norm_low = norm_params.astype(BF16).reshape(8, depth)

    def joined(pack):
        return pack.reshape(tens, width, pack.shape[-1])

    if fast:
        norm_pack = jnp.pad(norm_low, ((0, 8), (0, 128 - depth)))
        (first_narrow,), norm_all = gather_call([narrow[0]], norm_pack)
        norm_full = norm_all[:, :, :8, :depth].reshape(-1, 8, depth)
        attn_all = [joined(first_narrow), None]
        feed_all = [None, None]
    else:
        attn_all, feed_all = (
            [joined(lax.all_gather(pack, ("tensor", "dp"), axis=0)) for pack in packs]
            for packs in (narrow, wide)
        )
        norm_full = lax.all_gather(norm_low, "dp", axis=0)
    norm_full = jnp.swapaxes(norm_full, 0, 1).reshape(2, 4, width).astype(F32)
    trig = angles(lax.dynamic_slice_in_dim(positions, tensor * rows, rows, 0))
    length = positions.shape[0]

    current = hidden_in
    saved = []
    kv = None
    for layer in range(2):
        norms = norm_full[layer]
        if layer == 0:
            qt, kv_here = qkv_call(True, current, norms, trig, attn_all[layer])
        else:
            (qt,) = qkv_call(False, current, norms, trig, attn_all[layer])
        if fast and layer == 0:
            at, lse, kv, feed = attend_call(
                qt, kv_here, length, [wide[layer]], share=True, ident=1
            )
            kv = kv.reshape(length, 2 * HD)
            feed_all[layer] = joined(feed)
        elif fast:
            at, lse, feed = attend_call(qt, kv, length, [wide[layer]], ident=4)
            feed_all[layer] = joined(feed)
        else:
            if layer == 0:
                kv = share_call(kv_here, tens).reshape(length, 2 * HD)
            at, lse = attend_call(qt, kv, length)
        if fast and layer == 0:
            after, act, slope, second = mix_call(
                current, norms, at, attn_all[layer], feed_all[layer], [narrow[1]], ident=2
            )
            attn_all[1] = joined(second)
        else:
            after, act, slope = mix_call(current, norms, at, attn_all[layer], feed_all[layer])
        saved.append((current, qt, at, lse, act, slope))
        current = after

    x, qt, at, lse, act, slope = saved[1]
    norms = norm_full[1]
    early, late = [None, None], [None, None]
    pack, dout, mlp = mix_back_call(
        out_grad, x, norms, at, act, slope, attn_all[1], feed_all[1]
    )
    if fast:
        gqt, dkv, early[1] = attend_back_call(qt, dout, at, lse, kv, trig, sent=pack, ident=5)
    else:
        gqt, dkv = attend_back_call(qt, dout, at, lse, kv, trig)
        early[1] = plain_scatter(pack, depth)
    grad, pack, sums = norm_back_call(False, out_grad, x, norms, mlp, gqt, attn_all[1])

    x, qt, at, lse, act, slope = saved[0]
    norms = norm_full[0]
    if fast:
        early_pack, dout, mlp, late[1] = mix_back_call(
            grad, x, norms, at, act, slope, attn_all[0], feed_all[0], pack, ident=6
        )
        gqt, dkv, early[0] = attend_back_call(
            qt, dout, at, lse, kv, trig, dkv, early_pack, True, ident=7
        )
    else:
        late[1] = plain_scatter(pack, depth)
        pack, dout, mlp = mix_back_call(
            grad, x, norms, at, act, slope, attn_all[0], feed_all[0]
        )
        early[0] = plain_scatter(pack, depth)
        gqt, dkv = attend_back_call(qt, dout, at, lse, kv, trig, dkv)
        dkv = merge_call(dkv)
    grad, pack = norm_back_call(
        True, grad, x, norms, mlp, gqt, attn_all[0], dkv, trig, sums
    )
    arrays = (
        (query_weight, query_first, query_second),
        (keyval_weight, keyval_first, keyval_second),
        (output_weight, output_first, output_second),
        (up_weight, up_first, up_second),
        (down_weight, down_first, down_second),
        (norm_params, norm_first, norm_second),
    )
    if fast:
        late[0], totals = norms_call(pack, early, late[1], arrays)
        *nexts, update_norms, trust_ratios = lamb_call(totals, early, late, arrays)
        return (current, grad, *nexts, update_norms[0, :17], trust_ratios[0, :17])
    late[0] = plain_scatter(pack, depth)
    hidden = up_weight.shape[2]
    query_g = jnp.stack([late[layer][:, :QW] for layer in range(2)])
    keyval_g = late[0][:, QW : QW + 2 * HD]
    output_g = jnp.stack([early[layer][:, 2 * hidden : 2 * hidden + QW].T for layer in range(2)])
    up_g = jnp.stack([early[layer][:, :hidden] for layer in range(2)])
    down_g = jnp.stack([early[layer][:, hidden : 2 * hidden].T for layer in range(2)])
    norm_g = late[0][:, QW + 2 * HD : QW + 2 * HD + 8].T.reshape(2, 4, depth)

    grads = (query_g, keyval_g, output_g, up_g, down_g, norm_g)
    parts = [lamb_parts(*array, grad) for array, grad in zip(arrays, grads)]
    updates = tuple((part[2] for part in parts))
    weight_total, update_total = lax.psum(
        (param_squares(masters, leader), param_squares(updates, leader)), ("dp", "tensor")
    )
    weight_norm = jnp.sqrt(weight_total)
    update_norms = jnp.sqrt(update_total)
    trust_ratios = weight_norm / update_norms
    nexts = apply_trust(masters, updates, trust_ratios)
    outs = [current, grad]
    for index in range(6):
        low = nexts[index].astype(BF16)
        outs += [parts[index][0], parts[index][1], nexts[index], low]
    return tuple(outs) + (update_norms, trust_ratios)


def solution(mesh):
    fast = mesh.shape["dp"] == 8 and mesh.shape["tensor"] == 4
    columns = P(None, "dp", "tensor")
    across = P(None, "tensor", "dp")
    flat = P("dp", None)
    norm = P(None, None, "dp")
    state = P(("dp", "tensor"), None)
    in_specs = (
        (state, state, P("dp"), columns, flat, across, columns, across, norm)
        + (columns, columns, flat, flat, across, across, columns, columns, across, across)
        + (norm, norm)
    )
    out_specs = (
        (state, state)
        + (columns,) * 4
        + (flat,) * 4
        + (across,) * 4
        + (columns,) * 4
        + (across,) * 4
        + (norm,) * 4
        + (P(), P())
    )
    return jax.shard_map(
        functools.partial(shards, fast),
        mesh=mesh,
        in_specs=in_specs,
        out_specs=out_specs,
        check_vma=False,
    )
```

time: 1760 us -> 480 us (0.27)
  waiting for transfers between devices: 743 us -> 0 us
  Pallas kernels: 0 us -> 448 us
  matrix products: 417 us -> 0 us
  blocking collectives: 183 us -> 0 us
  other arithmetic: 172 us -> 6.4 us
  local copies, waits for them, and re-layouts: 175 us -> 14.2 us
  loops' own time: 38.6 us -> 0 us
  between operations: 19.2 us -> 1.35 us
    pallas_call x0 -> x15, Pallas kernels: none -> 448 us  [the longest x2 146 us: attend_back_call(): pl.pallas_call(functools.partial(attend_back_kernel, before is not None,...]
    dot_general x91 -> x0, matrix products: 417 us -> none  [the longest x16 77.6 us: masked_scores(): jnp.einsum('qhd,kd->hqk', query_block, keys, preferred_element_type=jnp.f...]
    unnamed x25 -> x0, waiting for transfers between devices: 338 us -> none
    reduce_scatter x9 -> x0, waiting for transfers between devices: 325 us -> none  [the longest x2 112 us: shards(): lax.psum_scatter(term, 'tensor', scatter_dimension=0, tiled=True)]
    all_gather x4 -> x0, blocking collectives: 131 us -> none  [the longest x1 34.4 us: shards(): lax.all_gather(query_weight.astype(jnp.bfloat16), 'dp', axis=1, tiled=True)]
    reduce_sum x22 -> x0, other arithmetic: 83.2 us -> none  [the longest x8 54.2 us: one(): total = jnp.sum(weights, axis=-1, keepdims=True)]
    all_gather x8 -> x0, waiting for transfers between devices: 80.7 us -> none  [the longest x2 53.5 us: shards(): lax.all_gather(grad_state.astype(jnp.bfloat16), 'tensor', axis=0, tiled=T...]
    dynamic_update_slice x16 -> x0, local copies, waits for them, and re-layouts: 72.1 us -> none  [attention_backward(): lax.scan(one, (empty, empty), jnp.arange(length // block))]
  transfers between devices with their start and end apart: 21 -> 0, of which waited for: 14 -> 0; matrix products, arithmetic and copies ran while one was open for 30% -> 0% of each run, Pallas kernels for 0% -> 0%
where the time goes in v2:
time: 480 us; the launch traced here: 470 us
  Pallas kernels  448 us (93%)
  local copies, waits for them, and re-layouts  14.2 us (3%)
  other arithmetic  6.4 us (1%)
    pallas_call x2, Pallas kernels, attend_back_call(): pl.pallas_call(functools.partial(attend_back_kernel, before is not None,...  146 us
    pallas_call x2, Pallas kernels, attend_call(): pl.pallas_call(functools.partial(attend_kernel, share, len(packs)), grid=...  104 us
    pallas_call x2, Pallas kernels, mix_call(): pl.pallas_call(functools.partial(mix_kernel, len(packs)), grid=(tens,), i...  51.8 us
    pallas_call x2, Pallas kernels, mix_back_call(): pl.pallas_call(functools.partial(mix_back_kernel, int(sent is not None)),...  48 us
    pallas_call x1, Pallas kernels, norms_call(): pl.pallas_call(norms_kernel, in_specs=[pl.BlockSpec(memory_space=pl.ANY)]...  32.7 us
    pallas_call x1, Pallas kernels, gather_call(): pl.pallas_call(functools.partial(gather_kernel, count), in_specs=[anywher...  28.3 us
    pallas_call x2, Pallas kernels, norm_back_call(): pl.pallas_call(functools.partial(norm_back_kernel, first), grid=(tens,),...  19.7 us
    pallas_call x2, Pallas kernels, qkv_call(): pl.pallas_call(functools.partial(qkv_kernel, first), grid=(tens,), in_spe...  11.3 us

profile of v2, /device:TPU:0, one launch (start us, length us, event | category | flops | bytes accessed | tf_op | source)
XLA Modules:
  0.0 470.3 jit_solution(2386959512663168147)
XLA Ops:
  0.7 0.8 convert.49
  1.6 1.0 copy.60
  2.6 0.9 convert.48
  3.6 0.8 pad_maximum_fusion.2
  4.4 0.7 convert_element_type.29
  5.7 28.3 %shard_map.420 = (bf16[4,4,2,96,512]{4,3,2,1,0:T(8,128)(2,1)}, bf16[2,4,16,128]{3,2,1,0:T(8,128)(2,1)}) custom-call(bf16[96,512]{1,0:T(8,128)(2,1)} %get-tuple-element.226.refs_0_, bf16[16,128]{1,0:T(8,128)(2,1)} %pad.4.refs_1_), custom_call_target="tpu_custom_call" | custom-call | tf_op jit(solution)/shard_map/pallas_call | solution.py:383
  34.0 0.7 slice_convert_fusion
  34.7 0.7 squeeze.48.norm_ref.refs_1_.refs_2_
  35.4 0.8 dynamic-slice_convert_fusion
  37.0 5.9 %shard_map.421 = (bf16[4,256,512]{2,1,0:T(8,128)(2,1)}, bf16[512,128]{1,0:T(8,128)(2,1)}) custom-call(bf16[512,768]{1,0:T(8,128)(2,1)} %x_ref.3, f32[4,768]{1,0:T(4,128)} %squeeze.48.norm_ref.refs_1_.refs_2_, f32[16,512]{1,0:T(8,128)} %pad_maximum_fusion.4.trig_ref.refs_5_.rest_2_, bf16[4,768,512]{2,1,0:T(8,128)(2,1)} %bitcast.50, bf16[4,768,512]{2,1,0:T(8,128)(2,1)} %bitcast.51), custom_call_target="tpu_custom_call" | custom-call | tf_op jit(solution)/shard_map/pallas_call | solution.py:549
  43.0 0.9 pad_maximum_fusion
  43.9 52.6 %shard_map.422 = (bf16[4,256,512]{2,1,0:T(8,128)(2,1)}, f32[4,8,512]{2,1,0:T(8,128)}, bf16[4,512,128]{2,1,0:T(8,128)(2,1)}, bf16[4,4,2,96,1536]{4,3,2,1,0:T(8,128)(2,1)}) custom-call(bf16[4,256,512]{2,1,0:T(8,128)(2,1)} %get-tuple-element.94.refs_0_, bf16[512,128]{1,0:T(8,128)(2,1)} %get-tuple-element.95.refs_1_, bf16[96,1536]{1,0:T(8,128)(2,1)} %get-tuple-element.228.refs_2_), custom_call_target="tpu_custom_call" | custom-call | tf_op jit(solution)/shard_map/pallas_call | solution.py:697
  96.5 35.2 %shard_map.423 = (f32[512,768]{1,0:T(8,128)}, bf16[4,512,768]{2,1,0:T(8,128)(2,1)}, bf16[4,512,768]{2,1,0:T(8,128)(2,1)}, bf16[4,4,2,96,512]{4,3,2,1,0:T(8,128)(2,1)}) custom-call(bf16[512,768]{1,0:T(8,128)(2,1)} %x_ref.3, f32[4,768]{1,0:T(4,128)} %squeeze.48.norm_ref.refs_1_.refs_2_, bf16[4,256,512]{2,1,0:T(8,128)(2,1)} %get-tuple-element.96.refs_2_.refs_3_, ...), custom_call_target="tpu_custom_call" | custom-call | tf_op jit(solution)/shard_map/pallas_call | solution.py:759
  131.7 0.7 squeeze.53.norm_ref.refs_1_.refs_2_
  132.4 5.4 %shard_map.424.refs_0_ = bf16[4,256,512]{2,1,0:T(8,128)(2,1)} custom-call(f32[512,768]{1,0:T(8,128)} %get-tuple-element.98.x_ref.refs_0_.refs_1_, f32[4,768]{1,0:T(4,128)} %squeeze.53.norm_ref.refs_1_.refs_2_, f32[16,512]{1,0:T(8,128)} %pad_maximum_fusion.4.trig_ref.refs_5_.rest_2_, bf16[4,768,512]{2,1,0:T(8,128)(2,1)} %bitcast.56), custom_call_target="tpu_custom_call" | custom-call | tf_op jit(solution)/shard_map/pallas_call | solution.py:549
  137.8 51.3 %shard_map.425 = (bf16[4,256,512]{2,1,0:T(8,128)(2,1)}, f32[4,8,512]{2,1,0:T(8,128)}, bf16[4,4,2,96,1536]{4,3,2,1,0:T(8,128)(2,1)}) custom-call(bf16[4,256,512]{2,1,0:T(8,128)(2,1)} %shard_map.424.refs_0_, bf16[2048,128]{1,0:T(8,128)(2,1)} %bitcast.62, bf16[96,1536]{1,0:T(8,128)(2,1)} %get-tuple-element.229.refs_2_), custom_call_target="tpu_custom_call" | custom-call | tf_op jit(solution)/shard_map/pallas_call | solution.py:697
  189.1 16.6 %shard_map.426 = (f32[512,768]{1,0:T(8,128)}, bf16[4,512,768]{2,1,0:T(8,128)(2,1)}, bf16[4,512,768]{2,1,0:T(8,128)(2,1)}) custom-call(f32[512,768]{1,0:T(8,128)} %get-tuple-element.98.x_ref.refs_0_.refs_1_, f32[4,768]{1,0:T(4,128)} %squeeze.53.norm_ref.refs_1_.refs_2_, bf16[4,256,512]{2,1,0:T(8,128)(2,1)} %get-tuple-element.101.refs_2_.refs_3_, ...), custom_call_target="tpu_custom_call" | custom-call | tf_op jit(solution)/shard_map/pallas_call | solution.py:759
  205.7 18.6 %shard_map.427 = (bf16[4,768,1792]{2,1,0:T(8,128)(2,1)}, bf16[4,256,512]{2,1,0:T(8,128)(2,1)}, f32[512,768]{1,0:T(8,128)}) custom-call(f32[512,768]{1,0:T(8,128)} %gx_ref.1, f32[512,768]{1,0:T(8,128)} %get-tuple-element.98.x_ref.refs_0_.refs_1_, f32[4,768]{1,0:T(4,128)} %squeeze.53.norm_ref.refs_1_.refs_2_, ...), custom_call_target="tpu_custom_call" | custom-call | tf_op jit(solution)/shard_map/pallas_call | solution.py:869
  224.4 78.4 %shard_map.428 = (bf16[4,256,512]{2,1,0:T(8,128)(2,1)}, f32[4,128,512]{2,1,0:T(8,128)}, f32[96,1792]{1,0:T(8,128)}) custom-call(bf16[4,256,512]{2,1,0:T(8,128)(2,1)} %shard_map.424.refs_0_, bf16[4,256,512]{2,1,0:T(8,128)(2,1)} %get-tuple-element.107.refs_1_, bf16[4,256,512]{2,1,0:T(8,128)(2,1)} %get-tuple-element.101.refs_2_.refs_3_, ...), custom_call_target="tpu_custom_call" | custom-call | tf_op jit(solution)/shard_map/pallas_call | solution.py:1042
  302.8 9.1 %shard_map.429 = (f32[512,768]{1,0:T(8,128)}, bf16[4,768,256]{2,1,0:T(8,128)(2,1)}, f32[4,768]{1,0:T(4,128)}) custom-call(f32[512,768]{1,0:T(8,128)} %gx_ref.1, f32[512,768]{1,0:T(8,128)} %get-tuple-element.98.x_ref.refs_0_.refs_1_, f32[4,768]{1,0:T(4,128)} %squeeze.53.norm_ref.refs_1_.refs_2_, f32[512,768]{1,0:T(8,128)} %get-tuple-element.106.mlp_ref, ...), custom_call_target="tpu_custom_call" | custom-call | tf_op jit(solution)/shard_map/pallas_call | solution.py:1131
  311.9 29.3 %shard_map.430 = (bf16[4,768,1792]{2,1,0:T(8,128)(2,1)}, bf16[4,256,512]{2,1,0:T(8,128)(2,1)}, f32[512,768]{1,0:T(8,128)}, f32[96,256]{1,0:T(8,128)}) custom-call(f32[512,768]{1,0:T(8,128)} %get-tuple-element.111.refs_0_.gx_ref, bf16[512,768]{1,0:T(8,128)(2,1)} %x_ref.3, f32[4,768]{1,0:T(4,128)} %squeeze.48.norm_ref.refs_1_.refs_2_, ...), custom_call_target="tpu_custom_call" | custom-call | tf_op jit(solution)/shard_map/pallas_call | solution.py:869
  341.3 67.3 %shard_map.431 = (bf16[4,256,512]{2,1,0:T(8,128)(2,1)}, f32[128,512]{1,0:T(8,128)}, f32[96,1792]{1,0:T(8,128)}) custom-call(bf16[4,256,512]{2,1,0:T(8,128)(2,1)} %get-tuple-element.94.refs_0_, bf16[4,256,512]{2,1,0:T(8,128)(2,1)} %get-tuple-element.116.refs_1_, bf16[4,256,512]{2,1,0:T(8,128)(2,1)} %get-tuple-element.96.refs_2_.refs_3_, ...), custom_call_target="tpu_custom_call" | custom-call | tf_op jit(solution)/shard_map/pallas_call | solution.py:1042
  408.6 10.6 %shard_map.432 = (f32[512,768]{1,0:T(8,128)}, bf16[4,768,384]{2,1,0:T(8,128)(2,1)}) custom-call(f32[512,768]{1,0:T(8,128)} %get-tuple-element.111.refs_0_.gx_ref, bf16[512,768]{1,0:T(8,128)(2,1)} %x_ref.3, f32[4,768]{1,0:T(4,128)} %squeeze.48.norm_ref.refs_1_.refs_2_, f32[512,768]{1,0:T(8,128)} %get-tuple-element.115.mlp_ref, ...), custom_call_target="tpu_custom_call" | custom-call | tf_op jit(solution)/shard_map/pallas_call | solution.py:1131
  419.2 1.2 copy.64.refs_16_.refs_17_
  420.4 1.2 copy.65.refs_17_.refs_18_
  421.6 1.2 copy.66.refs_18_.refs_19_
  422.7 32.7 %shard_map.433 = (f32[96,384]{1,0:T(8,128)}, f32[8,128]{1,0:T(8,128)}) custom-call(bf16[4,4,2,96,384]{4,3,2,1,0:T(8,128)(2,1)} %bitcast.65, f32[96,1792]{1,0:T(8,128)} %get-tuple-element.125.refs_1_, f32[96,1792]{1,0:T(8,128)} %get-tuple-element.126.refs_2_, f32[96,256]{1,0:T(8,128)} %get-tuple-element.127.refs_3_.refs_4_, f32[2,96,192]{2,1,0:T(8,128)} %refs_5_.3, ...), custom_call_target="tpu_custom_call" | custom-call | tf_op jit(solution)/shard_map/pallas_call | solution.py:1285
  455.4 6.9 %shard_map.434 = (f32[2,96,192]{2,1,0:T(8,128)}, f32[2,96,192]{2,1,0:T(8,128)}, f32[2,96,192]{2,1,0:T(8,128)}, bf16[2,96,192]{2,1,0:T(8,128)(2,1)}, f32[96,128]{...) custom-call(f32[8,128]{1,0:T(8,128)} %get-tuple-element.128.refs_0_,, ...), custom_call_target="tpu_custom_call" | custom-call | tf_op jit(solution)/shard_map/pallas_call | solution.py:1339
  462.4 2.3 copy.70
  464.7 2.2 copy.71
  466.9 1.1 copy.72
  468.0 0.9 copy.73
  (34 shorter events, 2.7 us)
Async XLA Ops:
  36.9 5.9 %copy-start.1 = (f32[2,768,96]{1,2,0:T(8,128)S(1)}, f32[2,768,96]{1,2,0:T(8,128)}, u32[]{:S(2)}) copy-start(f32[2,768,96]{1,2,0:T(8,128)} %param.28) | copy-start | bytes 1769476
  37.0 6.0 %copy-start = (f32[2,96,768]{2,1,0:T(8,128)S(1)}, f32[2,96,768]{2,1,0:T(8,128)}, u32[]{:S(2)}) copy-start(f32[2,96,768]{2,1,0:T(8,128)} %refs_14_.3) | copy-start | bytes 1769476
  408.6 11.8 %copy-start.3 = (f32[2,768,96]{1,2,0:T(8,128)S(1)}, f32[2,768,96]{1,2,0:T(8,128)}, u32[]{:S(2)}) copy-start(f32[2,768,96]{1,2,0:T(8,128)} %param.38) | copy-start | bytes 1769476
  419.2 2.3 copy-start.4
  462.3 4.5 copy-start.2
  462.3 5.6 %copy-start.5 = (bf16[2,768,96]{2,1,0:T(8,128)(2,1)S(1)}, bf16[2,768,96]{2,1,0:T(8,128)(2,1)}, u32[]{:S(2)}) copy-start(bf16[2,768,96]{2,1,0:T(8,128)(2,1)} %get-tuple-element.205) | copy-start | bytes 884740
  462.4 6.5 %copy-start.7 = (f32[1,128]{1,0:T(1,128)S(1)}, f32[1,128]{1,0:T(1,128)}, u32[]{:S(2)}) copy-start(f32[1,128]{1,0:T(1,128)} %get-tuple-element.154) | copy-start | bytes 1540
  462.4 7.0 %copy-start.6 = (f32[1,128]{1,0:T(1,128)S(1)}, f32[1,128]{1,0:T(1,128)}, u32[]{:S(2)}) copy-start(f32[1,128]{1,0:T(1,128)} %get-tuple-element.155) | copy-start | bytes 1540
